TPU v7x, 32 devices: a whole 2x2x4 slice. The times are simulated.
32 devices in a mesh: section: 2 (over core), dp: 4 (over z), tp: 4 (over y, x).
Axes of the slice: x: 2, y: 2, z: 4, core: 2. Of those that a mesh axis runs over, the one named last changes fastest.
Arguments:
- section_in: float32 [2, 1536, 640], P('section', ('dp', 'tp')), may hold values from -6 to 6
- seq_lengths: int32 [12], P('dp'), may hold values from 0 to 384, as said below
- attn_norm: float32 [2, 640], P('section'), may hold values from 0.25 to 1.75
- q_norm: float32 [2, 256], P('section'), may hold values from 0.55 to 1.45
- k_norm: float32 [2, 256], P('section'), may hold values from 0.55 to 1.45
- w_query: bfloat16 [2, 640, 1024], P('section', None, 'tp'), may hold values from -0.25 to 0.25
- w_key: bfloat16 [2, 640, 256], P('section', None, 'tp'), may hold values from -0.25 to 0.25
- w_value: bfloat16 [2, 640, 256], P('section', None, 'tp'), may hold values from -0.25 to 0.25
- w_out: bfloat16 [2, 1024, 640], P('section', 'tp'), may hold values from -0.1875 to 0.1875
- post_attn_norm: float32 [2, 640], P('section'), may hold values from 0.25 to 1.75
- ff_norm: float32 [2, 640], P('section'), may hold values from 0.25 to 1.75
- w_gate: bfloat16 [2, 640, 2048], P('section', None, 'tp'), may hold values from -0.25 to 0.25
- w_up: bfloat16 [2, 640, 2048], P('section', None, 'tp'), may hold values from -0.25 to 0.25
- w_down: bfloat16 [2, 2048, 640], P('section', 'tp'), may hold values from -0.125 to 0.125
- post_ff_norm: float32 [2, 640], P('section'), may hold values from 0.25 to 1.75
Outputs:
- section_out: float32 [2, 1536, 640], P('section', ('dp', 'tp'))
- attn_norm_grad: float32 [2, 640], P('section')
- q_norm_grad: float32 [2, 256], P('section')
- k_norm_grad: float32 [2, 256], P('section')
- w_query_grad: float32 [2, 640, 1024], P('section', None, 'tp')
- w_key_grad: float32 [2, 640, 256], P('section', None, 'tp')
- w_value_grad: float32 [2, 640, 256], P('section', None, 'tp')
- w_out_grad: float32 [2, 1024, 640], P('section', 'tp')
- post_attn_norm_grad: float32 [2, 640], P('section')
- ff_norm_grad: float32 [2, 640], P('section')
- w_gate_grad: float32 [2, 640, 2048], P('section', None, 'tp')
- w_up_grad: float32 [2, 640, 2048], P('section', None, 'tp')
- w_down_grad: float32 [2, 2048, 640], P('section', 'tp')
- post_ff_norm_grad: float32 [2, 640], P('section')
Inputs may be any that keep to these rules, and one draw needn't show every extreme that they name: `seq_lengths`: in each group of 3 slots, the lengths rounded up to multiples of 128 add up to at most 384; some slot has length exactly 384.
All inputs are finite; a program needn't handle non-finite values.
Results may differ from a plain program's by a relative error of at most 0.025.
Values may be sent and summed in bfloat16 or wider, within the bound.
A program may use at most 128 MiB of HBM per device.

v0:
```python
import jax
import jax.numpy as jnp
from jax import lax
from jax.sharding import PartitionSpec as P

WINDOW = 512
BLOCK = 128
QBLOCK = 1024


EPSILON = 1e-06


def passed_along(value, axis, steps):
    count = lax.axis_size(axis)
    pairs = [(source, (source + steps) % count) for source in range(count)]
    return lax.ppermute(value, axis, pairs)


def norm_stats(values):
    inverse = lax.rsqrt(jnp.mean(values * values, axis=-1, keepdims=True) + EPSILON)
    return (values * inverse, inverse)


def norm_back(normed, inverse, norm_gain, upstream):
    scaled = upstream * norm_gain
    result = inverse * (scaled - normed * jnp.mean(scaled * normed, axis=-1, keepdims=True))
    gain_grad = jnp.sum((upstream * normed).reshape(-1, normed.shape[-1]), axis=0)
    return (result, gain_grad)


def rotate(values, cos_table, sin_table):
    half_width = values.shape[-1] // 2
    leading = values[..., :half_width]
    trailing = values[..., half_width:]
    return jnp.concatenate(
        [leading * cos_table - trailing * sin_table, trailing * cos_table + leading * sin_table],
        axis=-1,
    )


def rotate_back(upstream, cos_table, sin_table):
    half_width = upstream.shape[-1] // 2
    leading = upstream[..., :half_width]
    trailing = upstream[..., half_width:]
    return jnp.concatenate(
        [leading * cos_table + trailing * sin_table, trailing * cos_table - leading * sin_table],
        axis=-1,
    )


def layout(lengths, row_count):
    slot_count = lengths.shape[0]
    padded = (lengths + (BLOCK - 1)) // BLOCK * BLOCK
    seq_ends = jnp.cumsum(padded)
    offsets = jnp.arange(row_count, dtype=jnp.int32)
    segment = jnp.sum((offsets[:, None] >= seq_ends[None, :]).astype(jnp.int32), axis=1)
    seq_starts = jnp.concatenate([jnp.zeros((1,), jnp.int32), seq_ends])
    extended = jnp.concatenate([lengths, jnp.zeros((1,), jnp.int32)])
    chosen = segment[:, None] == jnp.arange(slot_count + 1, dtype=jnp.int32)[None, :]
    seq_start = jnp.sum(jnp.where(chosen, seq_starts[None, :], 0), axis=1)
    seq_length = jnp.sum(jnp.where(chosen, extended[None, :], 0), axis=1)
    position = offsets - seq_start
    return (segment, position, position < seq_length)


def tables(position, rope_base, head_width):
    half_width = head_width // 2
    exponent = jnp.arange(half_width, dtype=jnp.float32) * (2.0 / head_width)
    frequency = jnp.power(rope_base, -exponent)
    angles = position.astype(jnp.float32)[:, None] * frequency[None, :]
    return (jnp.cos(angles), jnp.sin(angles))


def allowed(seg_query, pos_query, seg_key, pos_key, window):
    distance = pos_query[:, None] - pos_key[None, :]
    return (seg_query[:, None] == seg_key[None, :]) & (distance >= 0) & (distance < window)


def key_pad(key_rows, values, segment, position, padding):
    if padding == 0:
        return (key_rows, values, segment, position)
    blank_rows = jnp.zeros((padding, key_rows.shape[1]), key_rows.dtype)
    return (
        jnp.concatenate([blank_rows, key_rows]),
        jnp.concatenate([blank_rows, values]),
        jnp.concatenate([jnp.full((padding,), -1, jnp.int32), segment]),
        jnp.concatenate([jnp.zeros((padding,), jnp.int32), position]),
    )


def block_plan(row_count):
    block_rows = min(QBLOCK, row_count)
    blocks = row_count // block_rows
    padding = block_rows if blocks > 1 else 0
    return (block_rows, blocks, padding)


def attend(queries, key_rows, values, segment, position, window):
    row_count, head_count, head_width = queries.shape
    block_rows, blocks, padding = block_plan(row_count)
    score_scale = head_width ** (-0.5)
    padded_keys, padded_values, key_segment, key_position = key_pad(
        key_rows, values, segment, position, padding
    )

    def one_block(block_index):
        visible = allowed(segment, position, key_segment, key_position, window)
        scores = score_scale * jnp.einsum(
            "qhd,kd->hqk", queries, padded_keys, preferred_element_type=jnp.float32
        )
        scores = jnp.where(visible[None], scores, -1e30)
        highest = jnp.max(scores, axis=-1, keepdims=True)
        weights = jnp.where(visible[None], jnp.exp(scores - highest), 0.0)
        totals = jnp.sum(weights, axis=-1, keepdims=True)
        probability = (weights / totals).astype(jnp.bfloat16)
        output = jnp.einsum(
            "hqk,kd->qhd", probability, padded_values, preferred_element_type=jnp.float32
        ).astype(jnp.bfloat16)
        log_total = jnp.transpose((highest + jnp.log(totals))[..., 0])
        return (output, log_total)

    outputs, log_totals = lax.map(one_block, jnp.arange(blocks, dtype=jnp.int32))
    return (
        outputs.reshape(row_count, head_count, head_width),
        log_totals.reshape(row_count, head_count),
    )


def attend_back(
    queries, key_rows, values, segment, position, window, attended, log_totals, attended_grad
):
    row_count, head_count, head_width = queries.shape
    block_rows, blocks, padding = block_plan(row_count)
    key_span = block_rows + padding
    score_scale = head_width ** (-0.5)
    padded_keys, padded_values, key_segment, key_position = key_pad(
        key_rows, values, segment, position, padding
    )

    def one_step(running, block_index):
        key_acc, value_acc = running
        row_start = block_index * block_rows
        query_block = lax.dynamic_slice_in_dim(queries, row_start, block_rows, 0)
        key_block = lax.dynamic_slice_in_dim(padded_keys, row_start, key_span, 0)
        value_block = lax.dynamic_slice_in_dim(padded_values, row_start, key_span, 0)
        visible = allowed(
            lax.dynamic_slice_in_dim(segment, row_start, block_rows, 0),
            lax.dynamic_slice_in_dim(position, row_start, block_rows, 0),
            lax.dynamic_slice_in_dim(key_segment, row_start, key_span, 0),
            lax.dynamic_slice_in_dim(key_position, row_start, key_span, 0),
            window,
        )
        scores = score_scale * jnp.einsum(
            "qhd,kd->hqk", query_block, key_block, preferred_element_type=jnp.float32
        )
        scores = jnp.where(visible[None], scores, -1e30)
        log_block = jnp.transpose(lax.dynamic_slice_in_dim(log_totals, row_start, block_rows, 0))[
            :, :, None
        ]
        probability = jnp.where(visible[None], jnp.exp(scores - log_block), 0.0)
        low_prob = probability.astype(jnp.bfloat16)
        grad_block = lax.dynamic_slice_in_dim(attended_grad, row_start, block_rows, 0)
        att_block = lax.dynamic_slice_in_dim(attended, row_start, block_rows, 0)
        prob_grad = jnp.einsum(
            "qhd,kd->hqk", grad_block, value_block, preferred_element_type=jnp.float32
        )
        delta = jnp.transpose(
            jnp.sum(grad_block.astype(jnp.float32) * att_block.astype(jnp.float32), axis=-1)
        )[:, :, None]
        score_grad = (probability * (prob_grad - delta)).astype(jnp.bfloat16)
        query_grad = score_scale * jnp.einsum(
            "hqk,kd->qhd", score_grad, key_block, preferred_element_type=jnp.float32
        )
        key_grad = score_scale * jnp.einsum(
            "hqk,qhd->kd", score_grad, query_block, preferred_element_type=jnp.float32
        )
        value_grad = jnp.einsum(
            "hqk,qhd->kd", low_prob, grad_block, preferred_element_type=jnp.float32
        )
        key_acc = lax.dynamic_update_slice_in_dim(
            key_acc,
            lax.dynamic_slice_in_dim(key_acc, row_start, key_span, 0) + key_grad,
            row_start,
            0,
        )
        value_acc = lax.dynamic_update_slice_in_dim(
            value_acc,
            lax.dynamic_slice_in_dim(value_acc, row_start, key_span, 0) + value_grad,
            row_start,
            0,
        )
        return ((key_acc, value_acc), query_grad)

    blank_acc = jnp.zeros((row_count + padding, head_width), jnp.float32)
    (key_acc, value_acc), query_grads = lax.scan(
        one_step, (blank_acc, blank_acc), jnp.arange(blocks, dtype=jnp.int32)
    )
    return (
        query_grads.reshape(row_count, head_count, head_width),
        key_acc[padding:],
        value_acc[padding:],
    )


def gelu_tanh(values):
    return jax.nn.gelu(values, approximate=True)


def gather_rows(values):
    return lax.all_gather(values, "tp", axis=0, tiled=True)


def sum_rows(values):
    return lax.psum_scatter(values, "tp", scatter_dimension=0, tiled=True)


def to_other(values):
    return passed_along(values, "section", 1)


def keep_as_is(values):
    return values


def by_section(first_section, former, latter):
    return jax.tree.map(
        lambda former_leaf, latter_leaf: jnp.where(first_section, former_leaf, latter_leaf),
        former,
        latter,
    )


def forward(hidden_in, params, context):
    (
        attn_gain,
        query_gain,
        key_gain,
        w_query,
        w_key,
        w_value,
        w_out,
        post_attn_gain,
        ff_gain,
        w_gate,
        w_up,
        w_down,
        post_ff_gain,
    ) = params
    segment, position, cos_table, sin_table, window = context
    head_width = query_gain.shape[0]
    head_count = w_query.shape[1] // head_width
    normed_in, inverse_in = norm_stats(hidden_in)
    attn_input = gather_rows((normed_in * attn_gain).astype(jnp.bfloat16))
    row_count = attn_input.shape[0]
    queries = jnp.dot(attn_input, w_query, preferred_element_type=jnp.float32).reshape(
        row_count, head_count, head_width
    )
    key_cols = jnp.dot(attn_input, w_key, preferred_element_type=jnp.float32).astype(jnp.bfloat16)
    value_cols = jnp.dot(attn_input, w_value, preferred_element_type=jnp.float32).astype(
        jnp.bfloat16
    )
    keys_raw, values = (
        lax.all_gather(key_cols, "tp", axis=1, tiled=True),
        lax.all_gather(value_cols, "tp", axis=1, tiled=True),
    )
    query_normed, query_inverse = norm_stats(queries)
    query_rot = rotate(query_normed * query_gain, cos_table[:, None], sin_table[:, None]).astype(
        jnp.bfloat16
    )
    key_normed, key_inverse = norm_stats(keys_raw.astype(jnp.float32))
    key_rot = rotate(key_normed * key_gain, cos_table, sin_table).astype(jnp.bfloat16)
    attended, log_totals = attend(query_rot, key_rot, values, segment, position, window)
    attn_flat = attended.reshape(row_count, head_count * head_width)
    attn_sum = sum_rows(jnp.dot(attn_flat, w_out, preferred_element_type=jnp.float32))
    out_normed, out_inverse = norm_stats(attn_sum)
    middle = hidden_in + out_normed * post_attn_gain
    mid_normed, mid_inverse = norm_stats(middle)
    ff_input = gather_rows((mid_normed * ff_gain).astype(jnp.bfloat16))
    gate_pre = jnp.dot(ff_input, w_gate, preferred_element_type=jnp.float32)
    upward = jnp.dot(ff_input, w_up, preferred_element_type=jnp.float32)
    active = gelu_tanh(gate_pre)
    hidden = (active * upward).astype(jnp.bfloat16)
    ff_sum = sum_rows(jnp.dot(hidden, w_down, preferred_element_type=jnp.float32))
    ff_normed, ff_inverse = norm_stats(ff_sum)
    result = middle + ff_normed * post_ff_gain
    stored = dict(
        normed_in=normed_in,
        inverse_in=inverse_in,
        attn_input=attn_input,
        query_normed=query_normed,
        query_inverse=query_inverse,
        key_normed=key_normed,
        key_inverse=key_inverse,
        query_rot=query_rot,
        key_rot=key_rot,
        values=values,
        attended=attended,
        log_totals=log_totals,
        attn_flat=attn_flat,
        out_normed=out_normed,
        out_inverse=out_inverse,
        mid_normed=mid_normed,
        mid_inverse=mid_inverse,
        ff_input=ff_input,
        gate_pre=gate_pre,
        upward=upward,
        active=active,
        hidden=hidden,
        ff_normed=ff_normed,
        ff_inverse=ff_inverse,
    )
    return (result, stored)


def backward(params, stored, upstream, context, finish):
    (
        attn_gain,
        query_gain,
        key_gain,
        w_query,
        w_key,
        w_value,
        w_out,
        post_attn_gain,
        ff_gain,
        w_gate,
        w_up,
        w_down,
        post_ff_gain,
    ) = params
    segment, position, cos_table, sin_table, window = context
    head_width = query_gain.shape[0]
    head_count = w_query.shape[1] // head_width
    ff_grad, post_ff_grad = norm_back(
        stored["ff_normed"], stored["ff_inverse"], post_ff_gain, upstream
    )
    ff_cot = gather_rows(ff_grad.astype(jnp.bfloat16))
    row_count = ff_cot.shape[0]
    hidden_grad = jnp.einsum("tc,fc->tf", ff_cot, w_down, preferred_element_type=jnp.float32)
    down_grad = jnp.einsum(
        "tf,tc->fc", stored["hidden"], ff_cot, preferred_element_type=jnp.float32
    )
    gelu_out, slope = jax.vjp(gelu_tanh, stored["gate_pre"])
    gate_low = slope(hidden_grad * stored["upward"])[0].astype(jnp.bfloat16)
    up_low = (hidden_grad * stored["active"]).astype(jnp.bfloat16)
    gate_wgrad = jnp.einsum(
        "tc,tf->cf", stored["ff_input"], gate_low, preferred_element_type=jnp.float32
    )
    up_wgrad = jnp.einsum(
        "tc,tf->cf", stored["ff_input"], up_low, preferred_element_type=jnp.float32
    )
    ff_input_grad = sum_rows(
        jnp.einsum("tf,cf->tc", gate_low, w_gate, preferred_element_type=jnp.float32)
        + jnp.einsum("tf,cf->tc", up_low, w_up, preferred_element_type=jnp.float32)
    )
    ff_grads = finish((gate_wgrad, up_wgrad, down_grad))
    mid_back, ff_gain_grad = norm_back(
        stored["mid_normed"], stored["mid_inverse"], ff_gain, ff_input_grad
    )
    middle_grad = upstream + mid_back
    attn_grad, post_attn_grad = norm_back(
        stored["out_normed"], stored["out_inverse"], post_attn_gain, middle_grad
    )
    attn_cot = gather_rows(attn_grad.astype(jnp.bfloat16))
    out_wgrad = jnp.einsum(
        "te,tc->ec", stored["attn_flat"], attn_cot, preferred_element_type=jnp.float32
    )
    attended_grad = (
        jnp.einsum("tc,ec->te", attn_cot, w_out, preferred_element_type=jnp.float32)
        .astype(jnp.bfloat16)
        .reshape(row_count, head_count, head_width)
    )
    query_rgrad, key_rgrad, value_grad = attend_back(
        stored["query_rot"],
        stored["key_rot"],
        stored["values"],
        segment,
        position,
        window,
        stored["attended"],
        stored["log_totals"],
        attended_grad,
    )
    query_back, query_gain_grad = norm_back(
        stored["query_normed"],
        stored["query_inverse"],
        query_gain,
        rotate_back(query_rgrad, cos_table[:, None], sin_table[:, None]),
    )
    key_back, key_gain_grad = norm_back(
        stored["key_normed"],
        stored["key_inverse"],
        key_gain,
        rotate_back(key_rgrad, cos_table, sin_table),
    )
    key_part, value_part = (
        lax.psum_scatter(key_back, "tp", scatter_dimension=1, tiled=True),
        lax.psum_scatter(value_grad, "tp", scatter_dimension=1, tiled=True),
    )
    query_low = query_back.astype(jnp.bfloat16).reshape(row_count, head_count * head_width)
    key_low = key_part.astype(jnp.bfloat16)
    value_low = value_part.astype(jnp.bfloat16)
    attn_input = stored["attn_input"]
    query_wgrad = jnp.einsum("tc,te->ce", attn_input, query_low, preferred_element_type=jnp.float32)
    key_wgrad = jnp.einsum("tc,te->ce", attn_input, key_low, preferred_element_type=jnp.float32)
    value_wgrad = jnp.einsum("tc,te->ce", attn_input, value_low, preferred_element_type=jnp.float32)
    input_grad = sum_rows(
        jnp.einsum("te,ce->tc", query_low, w_query, preferred_element_type=jnp.float32)
        + jnp.einsum("te,ce->tc", key_low, w_key, preferred_element_type=jnp.float32)
        + jnp.einsum("te,ce->tc", value_low, w_value, preferred_element_type=jnp.float32)
    )
    in_back, attn_gain_grad = norm_back(
        stored["normed_in"], stored["inverse_in"], attn_gain, input_grad
    )
    grads = (
        attn_gain_grad,
        query_gain_grad,
        key_gain_grad,
        query_wgrad,
        key_wgrad,
        value_wgrad,
        out_wgrad,
        post_attn_grad,
        ff_gain_grad,
        ff_grads[0],
        ff_grads[1],
        ff_grads[2],
        post_ff_grad,
    )
    return (grads, middle_grad + in_back)


def local(
    section_in,
    seq_lengths,
    attn_norm,
    q_norm,
    k_norm,
    w_query,
    w_key,
    w_value,
    w_out,
    post_attn_norm,
    ff_norm,
    w_gate,
    w_up,
    w_down,
    post_ff_norm,
):
    params = (
        attn_norm[0],
        q_norm[0],
        k_norm[0],
        w_query[0],
        w_key[0],
        w_value[0],
        w_out[0],
        post_attn_norm[0],
        ff_norm[0],
        w_gate[0],
        w_up[0],
        w_down[0],
        post_ff_norm[0],
    )
    first_section = lax.axis_index("section") == 0
    tp_count = lax.axis_size("tp")
    tp_index = lax.axis_index("tp")
    local_in = section_in[0]
    local_count = local_in.shape[0]
    row_count = local_count * tp_count
    segment, position, valid_rows = layout(seq_lengths, row_count)
    own_valid = lax.dynamic_slice_in_dim(valid_rows, tp_index * local_count, local_count, 0).astype(
        jnp.float32
    )[:, None]
    window = jnp.where(first_section, WINDOW, row_count + 1)
    rope_base = jnp.where(first_section, 10000.0, 1000000.0).astype(jnp.float32)
    cos_table, sin_table = tables(position, rope_base, q_norm.shape[-1])
    context = (segment, position, cos_table, sin_table, window)
    result_first, stored_first = forward(local_in, params, context)
    received = to_other(result_first)
    result_second, stored_second = forward(received, params, context)
    grads_second, back_second = backward(
        params, stored_second, local_in * own_valid, context, keep_as_is
    )
    returned = to_other(back_second)
    grads_first, back_first = backward(params, stored_first, returned, context, keep_as_is)
    chosen = by_section(
        first_section, grads_first[3:7] + grads_first[9:12], grads_second[3:7] + grads_second[9:12]
    )
    matrices = lax.psum(
        (chosen[0], chosen[1], chosen[2], chosen[3], chosen[4], chosen[5], chosen[6]), "dp"
    )
    gain_pick = by_section(
        first_section,
        (
            grads_first[0],
            grads_first[1],
            grads_first[2],
            grads_first[7],
            grads_first[8],
            grads_first[12],
        ),
        (
            grads_second[0],
            grads_second[1],
            grads_second[2],
            grads_second[7],
            grads_second[8],
            grads_second[12],
        ),
    )
    gain_grads = lax.psum(
        (gain_pick[0], gain_pick[1], gain_pick[2], gain_pick[3], gain_pick[4], gain_pick[5]),
        ("dp", "tp"),
    )
    section_out = jnp.where(first_section, back_first, result_second)[None]
    return (
        section_out,
        gain_grads[0][None],
        gain_grads[1][None],
        gain_grads[2][None],
        matrices[0][None],
        matrices[1][None],
        matrices[2][None],
        matrices[3][None],
        gain_grads[3][None],
        gain_grads[4][None],
        matrices[4][None],
        matrices[5][None],
        matrices[6][None],
        gain_grads[5][None],
    )


def solution(mesh):
    return jax.shard_map(
        local,
        mesh=mesh,
        in_specs=(
            P("section", ("dp", "tp"), None),
            P("dp"),
            P("section", None),
            P("section", None),
            P("section", None),
            P("section", None, "tp"),
            P("section", None, "tp"),
            P("section", None, "tp"),
            P("section", "tp", None),
            P("section", None),
            P("section", None),
            P("section", None, "tp"),
            P("section", None, "tp"),
            P("section", "tp", None),
            P("section", None),
        ),
        out_specs=(
            P("section", ("dp", "tp"), None),
            P("section", None),
            P("section", None),
            P("section", None),
            P("section", None, "tp"),
            P("section", None, "tp"),
            P("section", None, "tp"),
            P("section", "tp", None),
            P("section", None),
            P("section", None),
            P("section", None, "tp"),
            P("section", None, "tp"),
            P("section", "tp", None),
            P("section", None),
        ),
        check_vma=False,
    )
```

profile of v0, /device:TPU:0, one launch (start us, length us, event | category | flops | bytes accessed | tf_op | source)
XLA Modules:
  0.0 755.7 jit_solution(9855226787544689452)
XLA Ops:
  14.4 11.5 %all_gather.36 = bf16[384,640]{1,0:T(8,128)(2,1)S(1)} all-gather(bf16[96,640]{1,0:T(8,128)(2,1)S(1)} %multiply_convert_fusion.13), channel_id=1, replica_groups=mesh['section'=2,'dp'=4,'tp'=4] {'tp'}, dimensions={0}, use_global_device_ids=true | all-gather | bytes 614400 | tf_op jit(solution)/shard_map/all_gather | solution.py:211
  26.5 9.0 %all_gather.38 = bf16[384,256]{0,1:T(8,128)(2,1)S(1)} all-gather(bf16[384,64]{0,1:T(8,128)(2,1)S(1)} %convolution_convert_fusion.6), channel_id=1, replica_groups=mesh['section'=2,'dp'=4,'tp'=4] {'tp'}, dimensions={1}, use_global_device_ids=true | all-gather | bytes 245760 | tf_op jit(solution)/shard_map/all_gather | solution.py:264
  35.6 7.8 %all_gather.37 = bf16[384,256]{0,1:T(8,128)(2,1)S(1)} all-gather(bf16[384,64]{0,1:T(8,128)(2,1)S(1)} %convolution_convert_fusion.7), channel_id=1, replica_groups=mesh['section'=2,'dp'=4,'tp'=4] {'tp'}, dimensions={1}, use_global_device_ids=true | all-gather | bytes 245760 | tf_op jit(solution)/shard_map/all_gather | solution.py:265
  53.0 27.6 %reduce-scatter.13.cloned.1.call-done = f32[96,640]{1,0:T(8,128)} async-done(((f32[384,640]{1,0:T(8,128)}), f32[96,640]{1,0:T(8,128)}) %reduce-scatter.13.cloned.1.call-update) | async-done | bytes 245776 | tf_op jit(solution)/shard_map/reduce_scatter | solution.py:215
  83.0 10.0 %all_gather.39 = bf16[384,640]{1,0:T(8,128)(2,1)S(1)} all-gather(bf16[96,640]{1,0:T(8,128)(2,1)S(1)} %multiply_convert_fusion.12), channel_id=1, replica_groups=mesh['section'=2,'dp'=4,'tp'=4] {'tp'}, dimensions={0}, use_global_device_ids=true | all-gather | bytes 614400 | tf_op jit(solution)/shard_map/all_gather | solution.py:211
  96.4 27.3 %reduce-scatter.15.cloned.1.call-done = f32[96,640]{1,0:T(8,128)} async-done(((f32[384,640]{1,0:T(8,128)}), f32[96,640]{1,0:T(8,128)}) %reduce-scatter.15.cloned.1.call-update) | async-done | bytes 245776 | tf_op jit(solution)/shard_map/reduce_scatter | solution.py:215
  128.3 9.8 %all_gather.40 = bf16[384,640]{1,0:T(8,128)(2,1)S(1)} all-gather(bf16[96,640]{1,0:T(8,128)(2,1)S(1)} %multiply_convert_fusion.11), channel_id=1, replica_groups=mesh['section'=2,'dp'=4,'tp'=4] {'tp'}, dimensions={0}, use_global_device_ids=true | all-gather | bytes 614400 | tf_op jit(solution)/shard_map/all_gather | solution.py:211
  139.2 7.8 %all_gather.42 = bf16[384,256]{0,1:T(8,128)(2,1)S(1)} all-gather(bf16[384,64]{0,1:T(8,128)(2,1)S(1)} %convolution_convert_fusion.4), channel_id=1, replica_groups=mesh['section'=2,'dp'=4,'tp'=4] {'tp'}, dimensions={1}, use_global_device_ids=true | all-gather | bytes 245760 | tf_op jit(solution)/shard_map/all_gather | solution.py:264
  147.2 8.6 %all_gather.41 = bf16[384,256]{0,1:T(8,128)(2,1)S(1)} all-gather(bf16[384,64]{0,1:T(8,128)(2,1)S(1)} %convolution_convert_fusion.5), channel_id=1, replica_groups=mesh['section'=2,'dp'=4,'tp'=4] {'tp'}, dimensions={1}, use_global_device_ids=true | all-gather | bytes 245760 | tf_op jit(solution)/shard_map/all_gather | solution.py:265
  164.3 27.4 %reduce-scatter.17.cloned.1.call-done = f32[96,640]{1,0:T(8,128)} async-done(((f32[384,640]{1,0:T(8,128)}), f32[96,640]{1,0:T(8,128)}) %reduce-scatter.17.cloned.1.call-update) | async-done | bytes 245776 | tf_op jit(solution)/shard_map/reduce_scatter | solution.py:215
  194.7 10.2 %all_gather.43 = bf16[384,640]{1,0:T(8,128)(2,1)S(1)} all-gather(bf16[96,640]{1,0:T(8,128)(2,1)S(1)} %multiply_convert_fusion.10), channel_id=1, replica_groups=mesh['section'=2,'dp'=4,'tp'=4] {'tp'}, dimensions={0}, use_global_device_ids=true | all-gather | bytes 614400 | tf_op jit(solution)/shard_map/all_gather | solution.py:211
  210.3 26.1 %reduce-scatter.19.cloned.1.call-done = f32[96,640]{1,0:T(8,128)} async-done(((f32[384,640]{1,0:T(8,128)}), f32[96,640]{1,0:T(8,128)}) %reduce-scatter.19.cloned.1.call-update) | async-done | bytes 245776 | tf_op jit(solution)/shard_map/reduce_scatter | solution.py:215
  237.6 1.7 multiply_reduce_fusion.8
  240.3 9.8 %all_gather.44 = bf16[384,640]{1,0:T(8,128)(2,1)S(1)} all-gather(bf16[96,640]{1,0:T(8,128)(2,1)S(1)} %multiply_convert_fusion.9), channel_id=1, replica_groups=mesh['section'=2,'dp'=4,'tp'=4] {'tp'}, dimensions={0}, use_global_device_ids=true | all-gather | bytes 614400 | tf_op jit(solution)/shard_map/all_gather | solution.py:211
  256.1 26.1 %reduce-scatter.21.cloned.1.call-done = f32[96,640]{1,0:T(8,128)} async-done(((f32[384,640]{1,0:T(8,128)}), f32[96,640]{1,0:T(8,128)}) %reduce-scatter.21.cloned.1.call-update) | async-done | bytes 245776 | tf_op jit(solution)/shard_map/reduce_scatter | solution.py:215
  282.2 1.8 multiply_reduce_fusion.10
  284.0 2.0 multiply_reduce_fusion.12
  286.9 9.8 %all_gather.45 = bf16[384,640]{1,0:T(8,128)(2,1)S(1)} all-gather(bf16[96,640]{1,0:T(8,128)(2,1)S(1)} %multiply_convert_fusion.8), channel_id=1, replica_groups=mesh['section'=2,'dp'=4,'tp'=4] {'tp'}, dimensions={0}, use_global_device_ids=true | all-gather | bytes 614400 | tf_op jit(solution)/shard_map/all_gather | solution.py:211
  303.8 2.2 fusion.165
  306.0 2.0 fusion.103
  308.1 2.0 multiply_reduce_fusion
  313.3 13.6 %reduce-scatter.23.cloned.1.call-done = f32[384,64]{0,1:T(8,128)} async-done(((f32[384,256]{0,1:T(8,128)}), f32[384,64]{0,1:T(8,128)}) %reduce-scatter.23.cloned.1.call-update) | async-done | bytes 98320 | tf_op jit(solution)/shard_map/reduce_scatter | solution.py:398
  326.9 2.6 convolution_add_fusion.4
  329.4 25.2 %reduce-scatter.25.cloned.1.call-done = f32[384,64]{0,1:T(8,128)} async-done(((f32[384,256]{0,1:T(8,128)}), f32[384,64]{0,1:T(8,128)}) %reduce-scatter.25.cloned.1.call-update) | async-done | bytes 98320 | tf_op jit(solution)/shard_map/reduce_scatter | solution.py:399
  354.7 2.6 convolution_add_fusion.3
  357.3 28.2 %reduce-scatter.27.cloned.1.call-done = f32[96,640]{1,0:T(8,128)} async-done(((f32[384,640]{1,0:T(8,128)}), f32[96,640]{1,0:T(8,128)}) %reduce-scatter.27.cloned.1.call-update) | async-done | bytes 245776 | tf_op jit(solution)/shard_map/reduce_scatter | solution.py:215
  385.5 1.8 multiply_reduce_fusion.14
  391.2 9.8 %all_gather.46 = bf16[384,640]{1,0:T(8,128)(2,1)S(1)} all-gather(bf16[96,640]{1,0:T(8,128)(2,1)S(1)} %multiply_convert_fusion.7), channel_id=1, replica_groups=mesh['section'=2,'dp'=4,'tp'=4] {'tp'}, dimensions={0}, use_global_device_ids=true | all-gather | bytes 614400 | tf_op jit(solution)/shard_map/all_gather | solution.py:211
  406.0 2.7 fusion.216
  408.7 1.6 fusion.215
  410.3 1.6 fusion.214
  411.9 21.2 %reduce-scatter.29.cloned.1.call-done = f32[96,640]{1,0:T(8,128)} async-done(((f32[384,640]{1,0:T(8,128)}), f32[96,640]{1,0:T(8,128)}) %reduce-scatter.29.cloned.1.call-update) | async-done | bytes 245776 | tf_op jit(solution)/shard_map/reduce_scatter | solution.py:215
  436.0 10.0 %all_gather.47 = bf16[384,640]{1,0:T(8,128)(2,1)S(1)} all-gather(bf16[96,640]{1,0:T(8,128)(2,1)S(1)} %multiply_convert_fusion.6), channel_id=1, replica_groups=mesh['section'=2,'dp'=4,'tp'=4] {'tp'}, dimensions={0}, use_global_device_ids=true | all-gather | bytes 614400 | tf_op jit(solution)/shard_map/all_gather | solution.py:211
  448.3 1.5 fusion.154
  451.0 2.9 fusion.1
  454.3 1.5 fusion.169
  455.8 2.0 fusion.100
  460.3 15.2 %reduce-scatter.31.cloned.1.call-done = f32[384,64]{0,1:T(8,128)} async-done(((f32[384,256]{0,1:T(8,128)}), f32[384,64]{0,1:T(8,128)}) %reduce-scatter.31.cloned.1.call-update) | async-done | bytes 98320 | tf_op jit(solution)/shard_map/reduce_scatter | solution.py:398
  475.5 2.6 convolution_add_fusion.1
  478.1 25.2 %reduce-scatter.33.cloned.1.call-done = f32[384,64]{0,1:T(8,128)} async-done(((f32[384,256]{0,1:T(8,128)}), f32[384,64]{0,1:T(8,128)}) %reduce-scatter.33.cloned.1.call-update) | async-done | bytes 98320 | tf_op jit(solution)/shard_map/reduce_scatter | solution.py:399
  503.3 2.6 convolution_add_fusion
  506.0 3.1 fusion
  509.1 1.6 fusion.2
  517.7 15.7 %reduce-scatter.35.cloned.1.call-done = f32[96,640]{1,0:T(8,128)} async-done(((f32[384,640]{1,0:T(8,128)}), f32[96,640]{1,0:T(8,128)}) %reduce-scatter.35.cloned.1.call-update) | async-done | bytes 245776 | tf_op jit(solution)/shard_map/reduce_scatter | solution.py:215
  534.6 79.3 %all-reduce = (f32[1,640]{1,0:T(1,128)}, f32[1,256]{1,0:T(1,128)}, f32[1,256]{1,0:T(1,128)}, f32[1,640]{1,0:T(1,128)}, f32[1,640]{1,0:T(1,128)}, /*index=5*/f32[1,640]{1,0:T(1,128)}) all-reduce(f32[1,640]{1,0:T(1,128)S(1)} %broadcast_in_dim.193, f32[1,256]{1,0:T(1,128)S(1)} %bitcast.307, ...), channel_id=1, replica_groups=mesh['section'=2,'dp'=4,'tp'=4] {'dp','tp'}, use_global_device_ids=true, to_apply=%region_48.49 | all-reduce | flops 3072 | bytes 24576 | tf_op jit(solution)/shard_map/psum | solution.py:513
  614.0 1.8 select_bitcast_fusion
  615.8 124.5 %all-reduce.4.cloned.1.call-done = (f32[1,640,256]{2,1,0:T(8,128)}, f32[1,640,64]{1,2,0:T(8,128)}, f32[1,640,64]{1,2,0:T(8,128)}, f32[1,256,640]{2,1,0:T(8,128)}...) async-done(((f32[1,640,256]{2,1,0:T(8,128)}, f32[1,640,64]{1,2,0:T(8,128)}, f32[1,640,64]{1,2,0:T(8,128)}, f32[1,256,640]{2,1,0:T(8,128)}, ...) | async-done | bytes 5570576 | tf_op jit(solution)/shard_map/psum | solution.py:491
  740.2 2.1 copy.36
  (491 shorter events, 96.6 us)
Async XLA Ops:
  7.2 87.7 %copy-start = (bf16[1,512,640]{2,1,0:T(8,128)(2,1)S(1)}, bf16[1,512,640]{2,1,0:T(8,128)(2,1)}, u32[]{:S(2)}) copy-start(bf16[1,512,640]{2,1,0:T(8,128)(2,1)} %param.28) | copy-start | bytes 1966084
  7.2 18.7 %copy-start.66 = (bf16[1,640,64]{1,2,0:T(8,128)(2,1)S(1)}, bf16[1,640,64]{1,2,0:T(8,128)(2,1)}, u32[]{:S(2)}) copy-start(bf16[1,640,64]{1,2,0:T(8,128)(2,1)} %param.21) | copy-start | bytes 245764
  7.2 19.0 %copy-start.67 = (bf16[1,640,64]{1,2,0:T(8,128)(2,1)S(1)}, bf16[1,640,64]{1,2,0:T(8,128)(2,1)}, u32[]{:S(2)}) copy-start(bf16[1,640,64]{1,2,0:T(8,128)(2,1)} %param.22) | copy-start | bytes 245764
  7.2 73.4 %reduce-scatter.13.cloned.1.call-start = ((), (), s32[]{:S(2)}) async-start(), calls=%async_computation.12 | async-start | bytes 1228800 | tf_op jit(solution)/shard_map/reduce_scatter | solution.py:215
  7.3 148.6 %copy-start.124 = (f32[128]{0:T(128)}, f32[128]{0:T(128)S(1)}, u32[]{:S(2)}) copy-start(f32[128]{0:T(128)S(1)} %negate_power_fusion) | copy-start | bytes 1540
  9.3 26.2 %copy-start.143 = (f32[96]{0:T(128)}, f32[96]{0:T(128)S(1)}, u32[]{:S(2)}) copy-start(f32[96]{0:T(128)S(1)} %add_rsqrt_fusion.11) | copy-start | bytes 1156
  12.0 23.5 %copy-start.127 = (s32[384]{0:T(512)}, s32[384]{0:T(512)S(1)}, u32[]{:S(2)}) copy-start(s32[384]{0:T(512)S(1)} %get-tuple-element.158) | copy-start | bytes 4612
  13.3 374.0 %copy-start.103 = (f32[640]{0:T(1024)}, f32[640]{0:T(1024)S(1)}, u32[]{:S(2)}) copy-start(f32[640]{0:T(1024)S(1)} %reduce.20) | copy-start | bytes 7684
  14.4 28.9 %copy-start.17 = (bf16[1,640,256]{2,1,0:T(8,128)(2,1)S(1)}, bf16[1,640,256]{2,1,0:T(8,128)(2,1)}, u32[]{:S(2)}) copy-start(bf16[1,640,256]{2,1,0:T(8,128)(2,1)} %param.20) | copy-start | bytes 983044
  26.2 17.6 %copy-start.117 = (f32[1,256]{1,0:T(1,128)S(1)}, f32[1,256]{1,0:T(1,128)}, u32[]{:S(2)}) copy-start(f32[1,256]{1,0:T(1,128)} %param.19) | copy-start | bytes 3076
  51.5 30.2 %copy-start.1 = (f32[1,96,640]{2,1,0:T(8,128)S(1)}, f32[1,96,640]{2,1,0:T(8,128)}, u32[]{:S(2)}) copy-start(f32[1,96,640]{2,1,0:T(8,128)} %param.15) | copy-start | bytes 737284
  52.9 40.1 %copy-start.2 = (bf16[1,640,512]{2,1,0:T(8,128)(2,1)S(1)}, bf16[1,640,512]{2,1,0:T(8,128)(2,1)}, u32[]{:S(2)}) copy-start(bf16[1,640,512]{2,1,0:T(8,128)(2,1)} %param.26) | copy-start | bytes 1966084
  52.9 70.9 %reduce-scatter.15.cloned.1.call-start = ((), (), s32[]{:S(2)}) async-start(), calls=%async_computation.13 | async-start | bytes 1228800 | tf_op jit(solution)/shard_map/reduce_scatter | solution.py:215
  82.9 42.0 %copy-start.6 = (f32[96,640]{1,0:T(8,128)}, f32[96,640]{1,0:T(8,128)S(1)}, u32[]{:S(2)}) copy-start(f32[96,640]{1,0:T(8,128)S(1)} %get-tuple-element.190) | copy-start | bytes 737284
  96.4 95.3 %reduce-scatter.17.cloned.1.call-start = ((), (), s32[]{:S(2)}) async-start(), calls=%async_computation.14 | async-start | bytes 1228800 | tf_op jit(solution)/shard_map/reduce_scatter | solution.py:215
  96.4 294.6 %copy-start.105 = (f32[640]{0:T(1024)}, f32[640]{0:T(1024)S(1)}, u32[]{:S(2)}) copy-start(f32[640]{0:T(1024)S(1)} %reduce.23) | copy-start | bytes 7684
  126.0 1.6 collective-permute-start
  139.2 18.4 %copy-start.5 = (f32[384,256]{0,1:T(8,128)}, f32[384,256]{0,1:T(8,128)S(1)}, u32[]{:S(2)}) copy-start(f32[384,256]{0,1:T(8,128)S(1)} %get-tuple-element.220) | copy-start | bytes 1179652
  162.9 29.9 %copy-start.45 = (bf16[384,256]{0,1:T(8,128)(2,1)}, bf16[384,256]{0,1:T(8,128)(2,1)S(1)}, u32[]{:S(2)}) copy-start(bf16[384,256]{0,1:T(8,128)(2,1)S(1)} %fusion.22) | copy-start | bytes 589828
  162.9 29.9 %copy-start.11 = (f32[96,640]{1,0:T(8,128)S(1)}, f32[96,640]{1,0:T(8,128)}, u32[]{:S(2)}) copy-start(f32[96,640]{1,0:T(8,128)} %copy-done.10) | copy-start | bytes 737284
  164.2 72.1 %reduce-scatter.19.cloned.1.call-start = ((), (), s32[]{:S(2)}) async-start(), calls=%async_computation.15 | async-start | bytes 1228800 | tf_op jit(solution)/shard_map/reduce_scatter | solution.py:215
  209.0 73.2 %reduce-scatter.21.cloned.1.call-start = ((), (), s32[]{:S(2)}) async-start(), calls=%async_computation.16 | async-start | bytes 1228800 | tf_op jit(solution)/shard_map/reduce_scatter | solution.py:215
  254.8 72.1 %reduce-scatter.23.cloned.1.call-start = ((), (), s32[]{:S(2)}) async-start(), calls=%async_computation.17 | async-start | bytes 491520 | tf_op jit(solution)/shard_map/reduce_scatter | solution.py:398
  302.3 52.4 %reduce-scatter.25.cloned.1.call-start = ((), (), s32[]{:S(2)}) async-start(), calls=%async_computation.18 | async-start | bytes 491520 | tf_op jit(solution)/shard_map/reduce_scatter | solution.py:399
  308.0 77.5 %reduce-scatter.27.cloned.1.call-start = ((), (), s32[]{:S(2)}) async-start(), calls=%async_computation.19 | async-start | bytes 1228800 | tf_op jit(solution)/shard_map/reduce_scatter | solution.py:215
  329.4 56.1 %copy-start.150 = (f32[96]{0:T(128)S(1)}, f32[96]{0:T(128)}, u32[]{:S(2)}) copy-start(f32[96]{0:T(128)} %copy-done.149) | copy-start | bytes 1156
  357.2 33.1 %copy-start.148 = (f32[96]{0:T(128)S(1)}, f32[96]{0:T(128)}, u32[]{:S(2)}) copy-start(f32[96]{0:T(128)} %copy-done.147) | copy-start | bytes 1156
  357.3 75.8 %reduce-scatter.29.cloned.1.call-start = ((), (), s32[]{:S(2)}) async-start(), calls=%async_computation.20 | async-start | bytes 1228800 | tf_op jit(solution)/shard_map/reduce_scatter | solution.py:215
  388.8 1.6 collective-permute-start.1
  405.7 69.8 %reduce-scatter.31.cloned.1.call-start = ((), (), s32[]{:S(2)}) async-start(), calls=%async_computation.21 | async-start | bytes 491520 | tf_op jit(solution)/shard_map/reduce_scatter | solution.py:398
  410.3 22.8 %copy-start.7 = (f32[96,640]{1,0:T(8,128)S(1)}, f32[96,640]{1,0:T(8,128)}, u32[]{:S(2)}) copy-start(f32[96,640]{1,0:T(8,128)} %copy-done.6) | copy-start | bytes 737284
  410.3 22.8 %copy-start.142 = (f32[96]{0:T(128)S(1)}, f32[96]{0:T(128)}, u32[]{:S(2)}) copy-start(f32[96]{0:T(128)} %copy-done.141) | copy-start | bytes 1156
  410.3 24.0 %copy-start.140 = (f32[96]{0:T(128)S(1)}, f32[96]{0:T(128)}, u32[]{:S(2)}) copy-start(f32[96]{0:T(128)} %copy-done.139) | copy-start | bytes 1156
  411.9 24.0 %copy-start.29 = (f32[96,640]{1,0:T(8,128)S(1)}, f32[96,640]{1,0:T(8,128)}, u32[]{:S(2)}) copy-start(f32[96,640]{1,0:T(8,128)} %reduce-scatter.13.cloned.1.call-done) | copy-start | bytes 737284
  450.9 52.4 %reduce-scatter.33.cloned.1.call-start = ((), (), s32[]{:S(2)}) async-start(), calls=%async_computation.22 | async-start | bytes 491520 | tf_op jit(solution)/shard_map/reduce_scatter | solution.py:399
  457.8 75.6 %reduce-scatter.35.cloned.1.call-start = ((), (), s32[]{:S(2)}) async-start(), calls=%async_computation.23 | async-start | bytes 1228800 | tf_op jit(solution)/shard_map/reduce_scatter | solution.py:215
  460.3 43.1 %copy-start.69 = (bf16[1,640,64]{1,2,0:T(8,128)(2,1)S(1)}, bf16[1,640,64]{1,2,0:T(8,128)(2,1)}, u32[]{:S(2)}) copy-start(bf16[1,640,64]{1,2,0:T(8,128)(2,1)} %param.22) | copy-start | bytes 245764
  478.1 27.9 %copy-start.42 = (bf16[384,640]{1,0:T(8,128)(2,1)S(1)}, bf16[384,640]{1,0:T(8,128)(2,1)}, u32[]{:S(2)}) copy-start(bf16[384,640]{1,0:T(8,128)(2,1)} %copy-done.41) | copy-start | bytes 1474564
  478.1 27.9 %copy-start.56 = (bf16[384,512]{1,0:T(8,128)(2,1)S(1)}, bf16[384,512]{1,0:T(8,128)(2,1)}, u32[]{:S(2)}) copy-start(bf16[384,512]{1,0:T(8,128)(2,1)} %copy-done.55) | copy-start | bytes 1179652
  505.9 234.3 %all-reduce.4.cloned.1.call-start = ((), (), s32[]{:S(2)}) async-start(), calls=%async_computation.24 | async-start | bytes 11141120 | tf_op jit(solution)/shard_map/psum | solution.py:491
  516.9 16.5 %copy-start.104 = (f32[640]{0:T(1024)S(1)}, f32[640]{0:T(1024)}, u32[]{:S(2)}) copy-start(f32[640]{0:T(1024)} %copy-done.103) | copy-start | bytes 7684
  516.9 16.5 %copy-start.144 = (f32[96]{0:T(128)S(1)}, f32[96]{0:T(128)}, u32[]{:S(2)}) copy-start(f32[96]{0:T(128)} %copy-done.143) | copy-start | bytes 1156
  516.9 17.6 %copy-start.131 = (f32[640]{0:T(1024)S(1)}, f32[640]{0:T(1024)}, u32[]{:S(2)}) copy-start(f32[640]{0:T(1024)} %get-tuple-element.153) | copy-start | bytes 7684
  516.9 97.0 %copy-start.9 = (f32[96,640]{1,0:T(8,128)S(1)}, f32[96,640]{1,0:T(8,128)}, u32[]{:S(2)}) copy-start(f32[96,640]{1,0:T(8,128)} %copy-done.8) | copy-start | bytes 737284
  516.9 97.0 %copy-start.30 = (f32[96,640]{1,0:T(8,128)S(1)}, f32[96,640]{1,0:T(8,128)}, u32[]{:S(2)}) copy-start(f32[96,640]{1,0:T(8,128)} %reduce-scatter.19.cloned.1.call-done) | copy-start | bytes 737284
  517.0 97.0 %copy-start.38 = (f32[96,640]{1,0:T(8,128)S(1)}, f32[96,640]{1,0:T(8,128)}, u32[]{:S(2)}) copy-start(f32[96,640]{1,0:T(8,128)} %copy-done.37) | copy-start | bytes 737284
  517.0 97.0 %copy-start.106 = (f32[640]{0:T(1024)S(1)}, f32[640]{0:T(1024)}, u32[]{:S(2)}) copy-start(f32[640]{0:T(1024)} %copy-done.105) | copy-start | bytes 7684
  517.0 97.0 %copy-start.146 = (f32[96]{0:T(128)S(1)}, f32[96]{0:T(128)}, u32[]{:S(2)}) copy-start(f32[96]{0:T(128)} %copy-done.145) | copy-start | bytes 1156
  (128 other events, 537.4 us)
Sparse Core Ops, SparseCore 0:
  53.0 27.5 reduce-scatter.12
  96.5 27.2 reduce-scatter.14
  164.3 27.2 reduce-scatter.16
  209.1 27.2 reduce-scatter.18
  254.9 27.2 reduce-scatter.20
  302.4 24.4 reduce-scatter.22
  330.2 24.4 reduce-scatter.24
  358.2 27.2 reduce-scatter.26
  405.8 27.2 reduce-scatter.28
  451.0 24.4 reduce-scatter.30
  478.9 24.4 reduce-scatter.32
  506.1 27.2 reduce-scatter.34
  537.5 202.7 all-reduce.3
where the time goes:
time: 758 us; the launch traced here: 756 us
  waiting for transfers between devices  407 us (54%)
  blocking collectives  193 us (25%)
  matrix products  63 us (8%)
  other arithmetic  56.9 us (8%)
  local copies, waits for them, and re-layouts  18.8 us (2%)
  between operations  16.1 us (2%)
    reduce_scatter x8, waiting for transfers between devices, sum_rows(): return lax.psum_scatter(values, 'tp', scatter_dimension=0, tiled=True)  200 us
    psum x1, waiting for transfers between devices, local(): lax.psum((chosen[0], chosen[1], chosen[2], chosen[3], chosen[4], chosen[5...  124 us
    all_gather x8, blocking collectives, gather_rows(): return lax.all_gather(values, 'tp', axis=0, tiled=True)  80.9 us
    psum x1, blocking collectives, local(): lax.psum((gain_pick[0], gain_pick[1], gain_pick[2], gain_pick[3], gain_pi...  79.3 us
    reduce_scatter x2, waiting for transfers between devices, backward(): lax.psum_scatter(value_grad, 'tp', scatter_dimension=1, tiled=True)  50.4 us
    reduce_scatter x2, waiting for transfers between devices, backward(): lax.psum_scatter(key_back, 'tp', scatter_dimension=1, tiled=True)  28.8 us
    unnamed x329, local copies, waits for them, and re-layouts  18.8 us
    all_gather x2, blocking collectives, forward(): lax.all_gather(key_cols, 'tp', axis=1, tiled=True)  16.8 us
  transfers between devices with their start and end apart: 15, of which 15 were waited for; matrix products, arithmetic and copies ran while one was open for 6% of the time, Pallas kernels for 0%

commit v1 on v0

v1 whole, which is shorter than its diff:
```python
import functools

import jax
import jax.numpy as jnp
from jax import lax
from jax.experimental import pallas as pl
from jax.experimental.pallas import tpu as pltpu
from jax.sharding import PartitionSpec as P

WINDOW = 512
BLOCK = 128
EPSILON = 1e-06
F32 = jnp.float32
BF16 = jnp.bfloat16
MESH = pl.DeviceIdType.MESH


def layout(lengths, row_count):
    slot_count = lengths.shape[0]
    padded = (lengths + (BLOCK - 1)) // BLOCK * BLOCK
    slots = jnp.arange(slot_count)
    seq_ends = jnp.sum(jnp.where(slots[:, None] <= slots[None, :], padded[:, None], 0), axis=0)
    offsets = jnp.arange(row_count, dtype=jnp.int32)
    segment = jnp.sum((offsets[:, None] >= seq_ends[None, :]).astype(jnp.int32), axis=1)
    seq_starts = jnp.concatenate([jnp.zeros((1,), jnp.int32), seq_ends])
    extended = jnp.concatenate([lengths, jnp.zeros((1,), jnp.int32)])
    chosen = segment[:, None] == jnp.arange(slot_count + 1, dtype=jnp.int32)[None, :]
    seq_start = jnp.sum(jnp.where(chosen, seq_starts[None, :], 0), axis=1)
    seq_length = jnp.sum(jnp.where(chosen, extended[None, :], 0), axis=1)
    position = offsets - seq_start
    return (segment, position, position < seq_length)


def tables(position, rope_base, head_width):
    half_width = head_width // 2
    exponent = jnp.arange(half_width, dtype=jnp.float32) * (2.0 / head_width)
    frequency = jnp.power(rope_base, -exponent)
    angles = position.astype(jnp.float32)[:, None] * frequency[None, :]
    return (jnp.cos(angles), jnp.sin(angles))


def stats(values):
    inverse = lax.rsqrt(jnp.mean(values * values, axis=-1, keepdims=True) + EPSILON)
    return values * inverse, inverse


def norm_back(normed, inverse, gain, upstream):
    scaled = upstream * gain
    result = inverse * (scaled - normed * jnp.mean(scaled * normed, axis=-1, keepdims=True))
    return result, jnp.sum(upstream * normed, axis=0, keepdims=True)


def rotate(values, cos, sin):
    half = values.shape[-1] // 2
    lead, trail = values[:, :half], values[:, half:]
    return jnp.concatenate([lead * cos - trail * sin, trail * cos + lead * sin], axis=-1)


def rotate_back(values, cos, sin):
    half = values.shape[-1] // 2
    lead, trail = values[:, :half], values[:, half:]
    return jnp.concatenate([lead * cos + trail * sin, trail * cos - lead * sin], axis=-1)


def dot(x, y):
    return jnp.dot(x, y, preferred_element_type=F32)


def dot_nt(x, y):
    return lax.dot_general(x, y, (((1,), (1,)), ((), ())), preferred_element_type=F32)


def dot_tn(x, y):
    return lax.dot_general(x, y, (((0,), (0,)), ((), ())), preferred_element_type=F32)


def layer_kernel(
    tp,
    x_ref, valid_ref, bias_ref, cos_ref, sin_ref,
    g_attn, g_q, g_k, wq, wk, wv, wo, g_pa, g_ff, wg, wu, wd, g_pf,
    sect_out, gains_out, dwq, dwk, dwv, dwo, dwg, dwu, dwd,
    wkv_all, wkf, wvf, hbuf, xbuf, sbuf,
    a_all, b_all, df_all, do_all,
    o_send, o_recv, f_send, f_recv, db_send, db_recv, da_send, da_recv, kv_send, kv_recv,
    qn_s, qi_s, kn_s, ki_s, qr_s, kr_s, v_s, p_s, att_s,
    gate_s, up_s, act_s, hid_s, slope_s, dgate_s, dup_s, dq_s, dk_s, dv_s, own_s, dmid_s,
    send_sem, recv_sem, x_send_sem, x_recv_sem,
):
    sec = lax.axis_index("section")
    me = lax.axis_index("tp")
    other = 1 - sec
    rows, width = x_ref.shape
    cols = wk.shape[1]
    scale = g_q.shape[1] ** (-0.5)
    peers = [lax.rem(me + k, tp) for k in range(tp)]
    mine = pl.ds(pl.multiple_of(me * rows, 16), rows)

    barrier = pltpu.get_barrier_semaphore()
    for k in range(1, tp):
        pl.semaphore_signal(barrier, inc=1, device_id={"tp": peers[k]}, device_id_type=MESH)
    pl.semaphore_signal(barrier, inc=1, device_id={"section": other}, device_id_type=MESH)
    pl.semaphore_wait(barrier, tp)

    pending = []

    def copy(ex, k, src, dst):
        return pltpu.make_async_remote_copy(
            src_ref=src, dst_ref=dst,
            send_sem=send_sem.at[ex, k - 1], recv_sem=recv_sem.at[ex, k - 1],
            device_id={"tp": peers[k]}, device_id_type=MESH,
        )

    def spread(ex, buf, where):
        copies = [copy(ex, k, buf.at[where], buf.at[where]) for k in range(1, tp)]
        for c in copies:
            c.start()
        pending.extend(copies)
        return copies

    def arrived(copies):
        for c in copies:
            c.wait_recv()

    def scatter(ex, send, recv, make):
        copies = []
        for k in range(1, tp):
            at = pl.ds(pl.multiple_of(peers[k] * rows, 16), rows)
            send[k - 1] = make(at).astype(BF16)
            c = copy(ex, k, send.at[k - 1], recv.at[k - 1])
            c.start()
            copies.append(c)
        own_s[...] = make(mine)
        pending.extend(copies)
        return copies

    def total(copies, recv):
        acc = own_s[...]
        for k in range(1, tp):
            copies[k - 1].wait_recv()
            acc = acc + recv[k - 1].astype(F32)
        return acc

    wkv_all[me] = jnp.concatenate([wk[...], wv[...]], axis=1)
    kvw = spread(0, wkv_all, me)

    cross = pltpu.make_async_remote_copy(
        src_ref=sbuf, dst_ref=xbuf, send_sem=x_send_sem, recv_sem=x_recv_sem,
        device_id={"section": other}, device_id_type=MESH,
    )

    arrived(kvw)
    for j in range(tp):
        block = wkv_all[j]
        wkf[:, j * cols:(j + 1) * cols] = block[:, :cols]
        wvf[:, j * cols:(j + 1) * cols] = block[:, cols:]

    @pl.when(sec == 0)
    def _():
        hbuf[...] = x_ref[...]

    @pl.when(sec == 1)
    def _():
        cross.wait_recv()
        hbuf[...] = xbuf[...]

    h = hbuf[...]
    n_in, i_in = stats(h)
    a_all[mine] = (n_in * g_attn[...]).astype(BF16)
    arrived(spread(1, a_all, mine))
    a = a_all[...]
    cos, sin = cos_ref[...], sin_ref[...]
    qn, qi = stats(dot(a, wq[...]))
    qn_s[...] = qn
    qi_s[...] = qi
    qr_s[...] = rotate(qn * g_q[...], cos, sin).astype(BF16)
    kn, ki = stats(dot(a, wkf[...]).astype(BF16).astype(F32))
    kn_s[...] = kn
    ki_s[...] = ki
    kr_s[...] = rotate(kn * g_k[...], cos, sin).astype(BF16)
    v_s[...] = dot(a, wvf[...]).astype(BF16)
    s = dot_nt(qr_s[...], kr_s[...]) * scale + bias_ref[...]
    e = jnp.exp(s - jnp.max(s, axis=-1, keepdims=True))
    p = e / jnp.sum(e, axis=-1, keepdims=True)
    p_s[...] = p
    att_s[...] = dot(p.astype(BF16), v_s[...]).astype(BF16)
    o_copies = scatter(2, o_send, o_recv, lambda at: dot(att_s[at], wo[...]))
    n_o, i_o = stats(total(o_copies, o_recv))
    mid = hbuf[...] + n_o * g_pa[...]
    n_mid, i_mid = stats(mid)
    b_all[mine] = (n_mid * g_ff[...]).astype(BF16)
    arrived(spread(3, b_all, mine))
    gate = dot(b_all[...], wg[...])
    up = dot(b_all[...], wu[...])
    gate_s[...] = gate
    up_s[...] = up
    c0 = 0.7978845608028654
    t = jnp.tanh(c0 * (gate + 0.044715 * gate * gate * gate))
    act = 0.5 * gate * (1.0 + t)
    act_s[...] = act
    hid_s[...] = (act * up).astype(BF16)
    slope_s[...] = t
    f_copies = scatter(4, f_send, f_recv, lambda at: dot(hid_s[at], wd[...]))
    gate = gate_s[...]
    t = slope_s[...]
    slope = 0.5 * (1.0 + t) + 0.5 * c0 * gate * (1.0 - t * t) * (1.0 + 3 * 0.044715 * gate * gate)
    slope_s[...] = slope * up_s[...]
    n_f, i_f = stats(total(f_copies, f_recv))
    out = mid + n_f * g_pf[...]

    @pl.when(sec == 0)
    def _():
        sbuf[...] = out
        cross.start()
        cross.wait_recv()
        hbuf[...] = xbuf[...]

    @pl.when(sec == 1)
    def _():
        sect_out[...] = out
        hbuf[...] = x_ref[...] * valid_ref[...]

    up_g = hbuf[...]
    df, dg_pf = norm_back(n_f, i_f, g_pf[...], up_g)
    df_all[mine] = df.astype(BF16)
    arrived(spread(5, df_all, mine))
    dhid = dot_nt(df_all[...], wd[...])
    dgate_s[...] = (dhid * slope_s[...]).astype(BF16)
    dup_s[...] = (dhid * act_s[...]).astype(BF16)
    db_copies = scatter(
        6, db_send, db_recv,
        lambda at: dot_nt(dgate_s[at], wg[...]) + dot_nt(dup_s[at], wu[...]),
    )
    dwd[...] = dot_tn(hid_s[...], df_all[...]).astype(dwd.dtype)
    db = total(db_copies, db_recv)
    mid_back, dg_ff = norm_back(n_mid, i_mid, g_ff[...], db)
    dmid = hbuf[...] + mid_back
    dmid_s[...] = dmid
    do, dg_pa = norm_back(n_o, i_o, g_pa[...], dmid)
    do_all[mine] = do.astype(BF16)
    do_copies = spread(7, do_all, mine)
    dwg[...] = dot_tn(b_all[...], dgate_s[...]).astype(dwg.dtype)
    arrived(do_copies)
    datt_f = dot_nt(do_all[...], wo[...])
    datt = datt_f.astype(BF16)
    delta = jnp.sum(datt.astype(F32) * att_s[...].astype(F32), axis=-1, keepdims=True)
    p = p_s[...]
    ds = (p * (dot_nt(datt, v_s[...]) - delta)).astype(BF16)
    dqr = dot(ds, kr_s[...]) * scale
    dkr = dot_tn(ds, qr_s[...]) * scale
    dv = dot_tn(p.astype(BF16), datt)
    dq, dg_q = norm_back(qn_s[...], qi_s[...], g_q[...], rotate_back(dqr, cos, sin))
    dk, dg_k = norm_back(kn_s[...], ki_s[...], g_k[...], rotate_back(dkr, cos, sin))
    dq_s[...] = dq.astype(BF16)
    dk_s[...] = dk.astype(BF16)
    dv_s[...] = dv.astype(BF16)
    da_copies = scatter(
        8, da_send, da_recv,
        lambda at: dot_nt(dq_s[at], wq[...]) + dot_nt(dk_s[at], wkf[...]) + dot_nt(dv_s[at], wvf[...]),
    )
    for j in range(tp):
        kv_send[j] = jnp.concatenate(
            [dk_s[:, j * cols:(j + 1) * cols], dv_s[:, j * cols:(j + 1) * cols]], axis=1
        )
    kv_copies = []
    for k in range(1, tp):
        c = copy(9, k, kv_send.at[peers[k]], kv_recv.at[k - 1])
        c.start()
        kv_copies.append(c)
    pending.extend(kv_copies)
    dwq[...] = dot_tn(a_all[...], dq_s[...]).astype(dwq.dtype)
    da = total(da_copies, da_recv)
    in_back, dg_attn = norm_back(n_in, i_in, g_attn[...], da)
    dh = dmid_s[...] + in_back

    @pl.when(sec == 1)
    def _():
        sbuf[...] = dh
        cross.start()

    @pl.when(sec == 0)
    def _():
        sect_out[...] = dh

    dwu[...] = dot_tn(b_all[...], dup_s[...]).astype(dwu.dtype)
    dwo[...] = dot_tn(att_s[...], do_all[...]).astype(dwo.dtype)
    dkv = kv_send[me].astype(F32)
    for k in range(1, tp):
        kv_copies[k - 1].wait_recv()
        dkv = dkv + kv_recv[k - 1].astype(F32)
    dwkv = dot_tn(a_all[...], dkv.astype(BF16))
    dwk[...] = dwkv[:, :cols].astype(dwk.dtype)
    dwv[...] = dwkv[:, cols:].astype(dwv.dtype)
    zero = jnp.zeros((1, width - dg_q.shape[1] - dg_k.shape[1]), F32)
    last = jnp.concatenate([dg_q, dg_k, zero], axis=1)
    gains_out[...] = jnp.concatenate(
        [dg_attn, dg_pa, dg_ff, dg_pf, last, jnp.zeros((3, width), F32)], axis=0
    )
    for c in pending:
        c.wait_send()
    cross.wait_send()


def local(
    section_in, seq_lengths, attn_norm, q_norm, k_norm, w_query, w_key, w_value, w_out,
    post_attn_norm, ff_norm, w_gate, w_up, w_down, post_ff_norm,
):
    first = lax.axis_index("section") == 0
    tp = lax.axis_size("tp")
    tp_index = lax.axis_index("tp")
    x = section_in[0]
    rows, width = x.shape
    n = rows * tp
    hd = q_norm.shape[-1]
    ff = w_gate.shape[2]
    cols = w_key.shape[2]
    segment, position, valid_rows = layout(seq_lengths, n)
    valid = lax.dynamic_slice_in_dim(valid_rows, tp_index * rows, rows, 0).astype(F32)[:, None]
    window = jnp.where(first, WINDOW, n + 1)
    rope_base = jnp.where(first, 10000.0, 1000000.0).astype(F32)
    cos, sin = tables(position, rope_base, hd)
    distance = position[:, None] - position[None, :]
    visible = (segment[:, None] == segment[None, :]) & (distance >= 0) & (distance < window)
    bias = jnp.where(visible, 0.0, -1e30).astype(F32)
    gt = BF16
    sds = jax.ShapeDtypeStruct
    vm = pltpu.VMEM
    rs = lambda: vm((tp - 1, rows, width), BF16)
    ag = lambda: vm((n, width), BF16)
    outs = pl.pallas_call(
        functools.partial(layer_kernel, tp),
        out_shape=[
            sds((rows, width), F32), sds((8, width), F32),
            sds((width, hd), gt), sds((width, cols), gt), sds((width, cols), gt),
            sds((hd, width), gt), sds((width, ff), gt), sds((width, ff), gt), sds((ff, width), gt),
        ],
        in_specs=[pl.BlockSpec(memory_space=pltpu.VMEM)] * 18,
        out_specs=[pl.BlockSpec(memory_space=pltpu.VMEM)] * 9,
        scratch_shapes=[
            vm((tp, width, 2 * cols), BF16), vm((width, hd), BF16), vm((width, hd), BF16),
            vm((rows, width), F32), vm((rows, width), F32), vm((rows, width), F32),
            ag(), ag(), ag(), ag(),
            rs(), rs(), rs(), rs(), rs(), rs(), rs(), rs(),
            vm((tp, n, 2 * cols), BF16), vm((tp - 1, n, 2 * cols), BF16),
            vm((n, hd), F32), vm((n, 1), F32), vm((n, hd), F32), vm((n, 1), F32),
            vm((n, hd), BF16), vm((n, hd), BF16), vm((n, hd), BF16), vm((n, n), F32), vm((n, hd), BF16),
            vm((n, ff), F32), vm((n, ff), F32), vm((n, ff), F32), vm((n, ff), BF16), vm((n, ff), F32),
            vm((n, ff), BF16), vm((n, ff), BF16), vm((n, hd), BF16), vm((n, hd), BF16), vm((n, hd), BF16),
            vm((rows, width), F32), vm((rows, width), F32),
            pltpu.SemaphoreType.DMA((10, tp - 1)), pltpu.SemaphoreType.DMA((10, tp - 1)),
            pltpu.SemaphoreType.DMA, pltpu.SemaphoreType.DMA,
        ],
        compiler_params=pltpu.CompilerParams(
            collective_id=0, has_side_effects=True, vmem_limit_bytes=56 * 1024 * 1024
        ),
    )(
        x, valid, bias, cos, sin, attn_norm, q_norm, k_norm, w_query[0], w_key[0], w_value[0],
        w_out[0], post_attn_norm, ff_norm, w_gate[0], w_up[0], w_down[0], post_ff_norm,
    )
    section_out, gains = outs[0], outs[1]
    gains = lax.psum(gains, ("dp", "tp"))
    mats = [m.astype(F32)[None] for m in lax.psum(tuple(outs[2:]), "dp")]
    row = lambda i: gains[i:i + 1]
    return (
        section_out[None], row(0), gains[4:5, :hd], gains[4:5, hd:2 * hd],
        mats[0], mats[1], mats[2], mats[3], row(1), row(2), mats[4], mats[5], mats[6], row(3),
    )


def solution(mesh):
    grid = P("section", None, "tp")
    down = P("section", "tp", None)
    gain = P("section", None)
    act = P("section", ("dp", "tp"), None)
    return jax.shard_map(
        local,
        mesh=mesh,
        in_specs=(
            act, P("dp"), gain, gain, gain, grid, grid, grid, down, gain, gain, grid, grid, down, gain,
        ),
        out_specs=(
            act, gain, gain, gain, grid, grid, grid, down, gain, gain, grid, grid, down, gain,
        ),
        check_vma=False,
    )
```

time: 758 us -> 267 us (0.35)
  waiting for transfers between devices: 407 us -> 36.8 us
  Pallas kernels: 0 us -> 117 us
  blocking collectives: 193 us -> 79.7 us
  matrix products: 63 us -> 0 us
  other arithmetic: 56.9 us -> 10.8 us
  local copies, waits for them, and re-layouts: 18.8 us -> 8.27 us
    reduce_scatter x12 -> x0, waiting for transfers between devices: 279 us -> none  [the longest x8 200 us: sum_rows(): return lax.psum_scatter(values, 'tp', scatter_dimension=0, tiled=True)]
    pallas_call x0 -> x1, Pallas kernels: none -> 117 us  [local(): pl.pallas_call(functools.partial(layer_kernel, tp), out_shape=[sds((rows,...]
    all_gather x12 -> x0, blocking collectives: 114 us -> none  [the longest x8 80.9 us: gather_rows(): return lax.all_gather(values, 'tp', axis=0, tiled=True)]
    psum x1, waiting for transfers between devices: 124 us -> 36.8 us  [local(): mats = [m.astype(F32)[None] for m in lax.psum(tuple(outs[2:]), 'dp')]]
    dot_general x54 -> x0, matrix products: 63 us -> none  [the longest x2 5.77 us: backward(): jnp.einsum('tf,tc->fc', stored['hidden'], ff_cot, preferred_element_type=...]
    reduce_sum x25 -> x2, other arithmetic: 26.5 us -> 0.18 us  [the longest x1 0.09 us: layout(): seq_start = jnp.sum(jnp.where(chosen, seq_starts[None, :], 0), axis=1)]
    unnamed x329 -> x21, local copies, waits for them, and re-layouts: 18.8 us -> 6.38 us
  transfers between devices with their start and end apart: 15 -> 1, of which waited for: 15 -> 1; matrix products, arithmetic and copies ran while one was open for 6% -> 0% of each run, Pallas kernels for 0% -> 0%
where the time goes in v1:
time: 267 us
  Pallas kernels  117 us (44%)
  blocking collectives  79.7 us (30%)
  waiting for transfers between devices  36.8 us (14%)
  between operations  14.1 us (5%)
  other arithmetic  10.8 us (4%)
  local copies, waits for them, and re-layouts  8.27 us (3%)
    pallas_call x1, Pallas kernels, local(): pl.pallas_call(functools.partial(layer_kernel, tp), out_shape=[sds((rows,...  117 us
    psum x1, blocking collectives, local(): gains = lax.psum(gains, ('dp', 'tp'))  79.7 us
    psum x1, waiting for transfers between devices, local(): mats = [m.astype(F32)[None] for m in lax.psum(tuple(outs[2:]), 'dp')]  36.8 us
    broadcast_in_dim x5, other arithmetic, local(): mats = [m.astype(F32)[None] for m in lax.psum(tuple(outs[2:]), 'dp')]  6.52 us
    unnamed x21, local copies, waits for them, and re-layouts  6.38 us
  transfers between devices with their start and end apart: 1, of which 1 were waited for; matrix products, arithmetic and copies ran while one was open for 0% of the time, Pallas kernels for 0%

profile of v1, /device:TPU:0, one launch (start us, length us, event | category | flops | bytes accessed | tf_op | source)
XLA Modules:
  0.0 266.7 jit_solution(15937691743630463855)
XLA Ops:
  7.2 0.0 all-reduce.3.cloned.1.call-start
  7.2 0.7 fusion.4
  7.9 0.1 select_reduce_fusion.2
  8.0 0.1 convert_reduce_fusion
  8.1 0.7 pad_add_fusion
  8.8 0.1 select_reduce_fusion.1
  8.9 0.1 fusion.3
  9.0 0.7 copy.36.valid_ref
  9.8 1.7 copy.34
  11.4 1.7 copy.35
  13.1 1.0 fusion.2.bias_ref
  14.2 1.5 multiply_sine_fusion
  15.7 117.0 %shard_map.254 = (f32[96,640]{1,0:T(8,128)}, f32[8,640]{1,0:T(8,128)}, bf16[640,256]{1,0:T(8,128)(2,1)}, bf16[640,64]{1,0:T(8,128)(2,1)}, bf16[640,64]{1,0:T(8,1...) custom-call(f32[96,640]{1,0:T(8,128)} %bitcast.30, ...), custom_call_target="tpu_custom_call" | custom-call | tf_op jit(solution)/shard_map/pallas_call | solution.py:329
  132.7 0.0 copy-start.7
  132.7 0.0 all-reduce.3.cloned.1.call-update
  132.7 0.7 copy-done.7
  133.4 79.7 %psum.56 = f32[8,640]{1,0:T(8,128)S(1)} all-reduce(f32[8,640]{1,0:T(8,128)S(1)} %copy-done.7), channel_id=1, replica_groups=mesh['section'=2,'dp'=4,'tp'=4] {'dp','tp'}, use_global_device_ids=true, to_apply=%region_4.5 | all-reduce | flops 5120 | bytes 40960 | tf_op jit(solution)/shard_map/psum | solution.py:360
  213.1 0.6 fusion.8
  213.6 0.6 fusion.7
  214.2 36.8 %all-reduce.3.cloned.1.call-done = (bf16[1,640,64]{2,1,0:T(8,128)(2,1)}, bf16[1,640,64]{2,1,0:T(8,128)(2,1)}, bf16[1,640,256]{2,1,0:T(8,128)(2,1)}, bf16[1,256,6...) async-done(((bf16[1,640,64]{2,1,0:T(8,128)(2,1)}, bf16[1,640,64]{2,1,0:T(8,128)(2,1)}, ...) | async-done | bytes 2785296 | tf_op jit(solution)/shard_map/psum | solution.py:361
  251.0 0.0 copy-start.1
  251.0 2.4 broadcast_in_dim.122
  253.4 0.0 copy-start
  253.4 0.0 copy-done.1
  253.4 1.2 broadcast_in_dim.124
  254.6 0.0 copy-start.3
  254.6 0.0 copy-done
  254.7 0.0 copy-start.2
  254.7 1.1 broadcast_in_dim.126
  255.8 0.0 copy-start.6
  255.8 0.0 copy-start.5
  255.8 0.0 copy-done.3
  255.8 0.0 copy-start.4
  255.8 0.9 broadcast_in_dim.114
  256.7 0.0 copy-done.2
  256.7 0.9 broadcast_in_dim.120
  257.6 0.0 copy-done.6
  257.6 0.8 copy.37
  258.4 0.0 copy-done.5
  258.4 0.8 copy.38
  259.2 0.0 copy-done.4
  259.2 0.7 copy.47
  (3 shorter events, 0.0 us)
Async XLA Ops:
  7.2 243.9 %all-reduce.3.cloned.1.call-start = ((), (), s32[]{:S(2)}) async-start(), calls=%async_computation | async-start | bytes 5898240 | tf_op jit(solution)/shard_map/psum | solution.py:361
  132.7 0.7 copy-start.7
  251.0 2.4 copy-start.1
  253.4 1.2 copy-start
  254.6 1.2 copy-start.3
  254.7 2.0 copy-start.2
  255.8 1.8 copy-start.6
  255.8 2.6 copy-start.5
  255.8 3.4 %copy-start.4 = (f32[96,640]{1,0:T(8,128)S(1)}, f32[96,640]{1,0:T(8,128)}, u32[]{:S(2)}) copy-start(f32[96,640]{1,0:T(8,128)} %get-tuple-element.23) | copy-start | bytes 737284
Sparse Core Ops, SparseCore 0:
  132.9 118.1 all-reduce.2

commit v2 on v1

--- a/solution.py
+++ b/solution.py
@@ -75,7 +75,7 @@
 
 
 def layer_kernel(
-    tp,
+    tp, dp, inside,
     x_ref, valid_ref, bias_ref, cos_ref, sin_ref,
     g_attn, g_q, g_k, wq, wk, wv, wo, g_pa, g_ff, wg, wu, wd, g_pf,
     sect_out, gains_out, dwq, dwk, dwv, dwo, dwg, dwu, dwd,
@@ -84,7 +84,7 @@
     o_send, o_recv, f_send, f_recv, db_send, db_recv, da_send, da_recv, kv_send, kv_recv,
     qn_s, qi_s, kn_s, ki_s, qr_s, kr_s, v_s, p_s, att_s,
     gate_s, up_s, act_s, hid_s, slope_s, dgate_s, dup_s, dq_s, dk_s, dv_s, own_s, dmid_s,
-    send_sem, recv_sem, x_send_sem, x_recv_sem,
+    send_sem, recv_sem, x_send_sem, x_recv_sem, *dp_refs,
 ):
     sec = lax.axis_index("section")
     me = lax.axis_index("tp")
@@ -99,7 +99,13 @@
     for k in range(1, tp):
         pl.semaphore_signal(barrier, inc=1, device_id={"tp": peers[k]}, device_id_type=MESH)
     pl.semaphore_signal(barrier, inc=1, device_id={"section": other}, device_id_type=MESH)
-    pl.semaphore_wait(barrier, tp)
+    if inside:
+        z = lax.axis_index("dp")
+        for k in range(1, dp):
+            pl.semaphore_signal(
+                barrier, inc=1, device_id={"dp": lax.rem(z + k, dp)}, device_id_type=MESH
+            )
+    pl.semaphore_wait(barrier, tp + (dp - 1 if inside else 0))
 
     pending = []
 
@@ -139,6 +145,60 @@
             copies[k - 1].wait_recv()
             acc = acc + recv[k - 1].astype(F32)
         return acc
+
+    if inside:
+        dkv_s, gain_tp, gain_dp, d_send, d_recv, g_send, g_recv = dp_refs[-7:]
+        low, high = lax.rem(z, 2), lax.rem(z // 2, 2)
+        near, far = z + 1 - 2 * low, z + 2 - 4 * high
+        grads = [dwd.at[0], dwg.at[0], dwu.at[0], dwo.at[0], dwq.at[0], dkv_s]
+        live = {}
+
+        def place(ref, start, size):
+            return ref.at[pl.ds(pl.multiple_of(start, 16), size)]
+
+        def move(i, step, src, dst, peer):
+            c = pltpu.make_async_remote_copy(
+                src_ref=src, dst_ref=dst, send_sem=d_send.at[i, step], recv_sem=d_recv.at[i, step],
+                device_id={"dp": peer}, device_id_type=MESH,
+            )
+            c.start()
+            pending.append(c)
+            live[i] = c
+
+        def advance(step, *which):
+            for i in which:
+                acc = grads[i]
+                first_out, first_in, second_out, second_in, whole = dp_refs[5 * i:5 * i + 5]
+                half, quarter = acc.shape[0] // 2, acc.shape[0] // 4
+                own_half = low * half
+                own_quarter = own_half + high * quarter
+                if step > 0:
+                    live[i].wait_recv()
+                if step == 0:
+                    first_out[...] = place(acc, (1 - low) * half, half)[...].astype(BF16)
+                    move(i, 0, first_out, first_in, near)
+                elif step == 1:
+                    kept = place(acc, own_half, half)
+                    kept[...] = kept[...] + first_in[...].astype(F32)
+                    second_out[...] = place(acc, own_half + (1 - high) * quarter, quarter)[...].astype(BF16)
+                    move(i, 1, second_out, second_in, far)
+                elif step == 2:
+                    done = place(whole, own_quarter, quarter)
+                    done[...] = (place(acc, own_quarter, quarter)[...] + second_in[...].astype(F32)).astype(BF16)
+                    move(i, 2, done, done, far)
+                elif step == 3:
+                    done = place(whole, own_half, half)
+                    move(i, 3, done, done, near)
+                elif i < 5:
+                    acc[...] = whole[...].astype(F32)
+                else:
+                    dwk[0] = whole[:, :cols].astype(F32)
+                    dwv[0] = whole[:, cols:].astype(F32)
+    else:
+        dkv_s = dp_refs[0]
+
+        def advance(step, *which):
+            pass
 
     wkv_all[me] = jnp.concatenate([wk[...], wv[...]], axis=1)
     kvw = spread(0, wkv_all, me)
@@ -230,7 +290,12 @@
         6, db_send, db_recv,
         lambda at: dot_nt(dgate_s[at], wg[...]) + dot_nt(dup_s[at], wu[...]),
     )
-    dwd[...] = dot_tn(hid_s[...], df_all[...]).astype(dwd.dtype)
+    dwd[0] = dot_tn(hid_s[...], df_all[...])
+    advance(0, 0)
+    dwg[0] = dot_tn(b_all[...], dgate_s[...])
+    advance(0, 1)
+    dwu[0] = dot_tn(b_all[...], dup_s[...])
+    advance(0, 2)
     db = total(db_copies, db_recv)
     mid_back, dg_ff = norm_back(n_mid, i_mid, g_ff[...], db)
     dmid = hbuf[...] + mid_back
@@ -238,7 +303,6 @@
     do, dg_pa = norm_back(n_o, i_o, g_pa[...], dmid)
     do_all[mine] = do.astype(BF16)
     do_copies = spread(7, do_all, mine)
-    dwg[...] = dot_tn(b_all[...], dgate_s[...]).astype(dwg.dtype)
     arrived(do_copies)
     datt_f = dot_nt(do_all[...], wo[...])
     datt = datt_f.astype(BF16)
@@ -267,7 +331,9 @@
         c.start()
         kv_copies.append(c)
     pending.extend(kv_copies)
-    dwq[...] = dot_tn(a_all[...], dq_s[...]).astype(dwq.dtype)
+    dwo[0] = dot_tn(att_s[...], do_all[...])
+    advance(0, 3)
+    advance(1, 0, 1, 2)
     da = total(da_copies, da_recv)
     in_back, dg_attn = norm_back(n_in, i_in, g_attn[...], da)
     dh = dmid_s[...] + in_back
@@ -281,20 +347,58 @@
     def _():
         sect_out[...] = dh
 
-    dwu[...] = dot_tn(b_all[...], dup_s[...]).astype(dwu.dtype)
-    dwo[...] = dot_tn(att_s[...], do_all[...]).astype(dwo.dtype)
+    zero = jnp.zeros((1, width - dg_q.shape[1] - dg_k.shape[1]), F32)
+    gains = jnp.concatenate(
+        [dg_attn, dg_pa, dg_ff, dg_pf, jnp.concatenate([dg_q, dg_k, zero], axis=1),
+         jnp.zeros((3, width), F32)], axis=0
+    )
+    gain_copies = []
+    if inside:
+        gain_tp[me] = gains
+        for k in range(1, tp):
+            c = pltpu.make_async_remote_copy(
+                src_ref=gain_tp.at[me], dst_ref=gain_tp.at[me], send_sem=g_send.at[0, k - 1],
+                recv_sem=g_recv.at[0, k - 1], device_id={"tp": peers[k]}, device_id_type=MESH,
+            )
+            c.start()
+            gain_copies.append(c)
+    else:
+        gains_out[...] = gains
+    dwq[0] = dot_tn(a_all[...], dq_s[...])
+    advance(0, 4)
     dkv = kv_send[me].astype(F32)
     for k in range(1, tp):
         kv_copies[k - 1].wait_recv()
         dkv = dkv + kv_recv[k - 1].astype(F32)
-    dwkv = dot_tn(a_all[...], dkv.astype(BF16))
-    dwk[...] = dwkv[:, :cols].astype(dwk.dtype)
-    dwv[...] = dwkv[:, cols:].astype(dwv.dtype)
-    zero = jnp.zeros((1, width - dg_q.shape[1] - dg_k.shape[1]), F32)
-    last = jnp.concatenate([dg_q, dg_k, zero], axis=1)
-    gains_out[...] = jnp.concatenate(
-        [dg_attn, dg_pa, dg_ff, dg_pf, last, jnp.zeros((3, width), F32)], axis=0
-    )
+    dkv_s[...] = dot_tn(a_all[...], dkv.astype(BF16))
+    advance(0, 5)
+    if inside:
+        advance(2, 0, 1, 2)
+        advance(1, 3)
+        for c in gain_copies:
+            c.wait_recv()
+        gain_dp[z] = sum(gain_tp[j] for j in range(tp))
+        more = []
+        for k in range(1, dp):
+            c = pltpu.make_async_remote_copy(
+                src_ref=gain_dp.at[z], dst_ref=gain_dp.at[z], send_sem=g_send.at[1, k - 1],
+                recv_sem=g_recv.at[1, k - 1], device_id={"dp": lax.rem(z + k, dp)},
+                device_id_type=MESH,
+            )
+            c.start()
+            more.append(c)
+        pending.extend(gain_copies + more)
+        advance(1, 4, 5)
+        advance(3, 0, 1, 2)
+        advance(2, 3, 4, 5)
+        advance(3, 3, 4, 5)
+        for c in more:
+            c.wait_recv()
+        gains_out[...] = sum(gain_dp[j] for j in range(dp))
+        advance(4, 0, 1, 2, 3, 4, 5)
+    else:
+        dwk[0] = dkv_s[:, :cols]
+        dwv[0] = dkv_s[:, cols:]
     for c in pending:
         c.wait_send()
     cross.wait_send()
@@ -321,17 +425,29 @@
     distance = position[:, None] - position[None, :]
     visible = (segment[:, None] == segment[None, :]) & (distance >= 0) & (distance < window)
     bias = jnp.where(visible, 0.0, -1e30).astype(F32)
-    gt = BF16
+    dp = lax.axis_size("dp")
+    inside = dp == 4 and width % 64 == 0 and hd % 64 == 0 and ff % 64 == 0
     sds = jax.ShapeDtypeStruct
     vm = pltpu.VMEM
     rs = lambda: vm((tp - 1, rows, width), BF16)
     ag = lambda: vm((n, width), BF16)
+    across = [vm((width, 2 * cols), F32)]
+    if inside:
+        across = []
+        for m, w in ((ff, width), (width, ff), (width, ff), (hd, width), (width, hd), (width, 2 * cols)):
+            across += [vm((m // 2, w), BF16)] * 2 + [vm((m // 4, w), BF16)] * 2 + [vm((m, w), BF16)]
+        sem = pltpu.SemaphoreType.DMA
+        across += [
+            vm((width, 2 * cols), F32), vm((tp, 8, width), F32), vm((dp, 8, width), F32),
+            sem((6, 4)), sem((6, 4)), sem((2, max(tp, dp) - 1)), sem((2, max(tp, dp) - 1)),
+        ]
     outs = pl.pallas_call(
-        functools.partial(layer_kernel, tp),
+        functools.partial(layer_kernel, tp, dp, inside),
         out_shape=[
             sds((rows, width), F32), sds((8, width), F32),
-            sds((width, hd), gt), sds((width, cols), gt), sds((width, cols), gt),
-            sds((hd, width), gt), sds((width, ff), gt), sds((width, ff), gt), sds((ff, width), gt),
+            sds((1, width, hd), F32), sds((1, width, cols), F32), sds((1, width, cols), F32),
+            sds((1, hd, width), F32), sds((1, width, ff), F32), sds((1, width, ff), F32),
+            sds((1, ff, width), F32),
         ],
         in_specs=[pl.BlockSpec(memory_space=pltpu.VMEM)] * 18,
         out_specs=[pl.BlockSpec(memory_space=pltpu.VMEM)] * 9,
@@ -348,7 +464,7 @@
             vm((rows, width), F32), vm((rows, width), F32),
             pltpu.SemaphoreType.DMA((10, tp - 1)), pltpu.SemaphoreType.DMA((10, tp - 1)),
             pltpu.SemaphoreType.DMA, pltpu.SemaphoreType.DMA,
-        ],
+        ] + across,
         compiler_params=pltpu.CompilerParams(
             collective_id=0, has_side_effects=True, vmem_limit_bytes=56 * 1024 * 1024
         ),
@@ -357,8 +473,10 @@
         w_out[0], post_attn_norm, ff_norm, w_gate[0], w_up[0], w_down[0], post_ff_norm,
     )
     section_out, gains = outs[0], outs[1]
-    gains = lax.psum(gains, ("dp", "tp"))
-    mats = [m.astype(F32)[None] for m in lax.psum(tuple(outs[2:]), "dp")]
+    mats = list(outs[2:])
+    if not inside:
+        gains = lax.psum(gains, ("dp", "tp"))
+        mats = [m.astype(F32) for m in lax.psum(tuple(m.astype(BF16) for m in mats), "dp")]
     row = lambda i: gains[i:i + 1]
     return (
         section_out[None], row(0), gains[4:5, :hd], gains[4:5, hd:2 * hd],

time: 267 us -> 198 us (0.74)
  blocking collectives: 79.7 us -> 0 us
  Pallas kernels: 117 us -> 174 us
  waiting for transfers between devices: 36.8 us -> 0 us
  between operations: 14.1 us -> 0.7 us
  local copies, waits for them, and re-layouts: 8.27 us -> 18.5 us
  other arithmetic: 10.8 us -> 4.31 us
    psum x1 -> x0, blocking collectives: 79.7 us -> none  [local(): gains = lax.psum(gains, ('dp', 'tp'))]
    pallas_call x1, Pallas kernels: 117 us -> 174 us  [local(): pl.pallas_call(functools.partial(layer_kernel, tp, dp, inside), out_shape...]
    psum x1 -> x0, waiting for transfers between devices: 36.8 us -> none  [local(): mats = [m.astype(F32)[None] for m in lax.psum(tuple(outs[2:]), 'dp')]]
    unnamed x21 -> x20, local copies, waits for them, and re-layouts: 6.38 us -> 15 us
    broadcast_in_dim x5 -> x0, other arithmetic: 6.52 us -> none  [local(): mats = [m.astype(F32)[None] for m in lax.psum(tuple(outs[2:]), 'dp')]]
  transfers between devices with their start and end apart: 1 -> 0, of which waited for: 1 -> 0; matrix products, arithmetic and copies ran while one was open for 0% -> 0% of each run, Pallas kernels for 0% -> 0%
where the time goes in v2:
time: 198 us; the launch traced here: 197 us
  Pallas kernels  174 us (88%)
  local copies, waits for them, and re-layouts  18.5 us (9%)
  other arithmetic  4.31 us (2%)
    pallas_call x1, Pallas kernels, local(): pl.pallas_call(functools.partial(layer_kernel, tp, dp, inside), out_shape...  174 us
    unnamed x20, local copies, waits for them, and re-layouts  15 us

profile of v2, /device:TPU:0, one launch (start us, length us, event | category | flops | bytes accessed | tf_op | source)
XLA Modules:
  0.0 197.1 jit_solution(119099955186831739)
XLA Ops:
  0.7 0.7 fusion.4
  1.4 0.1 select_reduce_fusion.2
  1.4 0.7 pad_add_fusion
  2.2 0.1 convert_reduce_fusion
  2.3 0.1 select_reduce_fusion.1
  2.4 0.1 fusion.3
  2.4 0.7 copy.36.valid_ref
  3.2 1.7 copy.34
  4.9 1.7 copy.35
  6.5 1.5 multiply_sine_fusion
  8.0 1.0 fusion.2.bias_ref
  9.1 173.6 %shard_map.254 = (f32[96,640]{1,0:T(8,128)}, f32[8,640]{1,0:T(8,128)}, f32[1,640,256]{2,1,0:T(8,128)}, f32[1,640,64]{2,1,0:T(8,128)}, f32[1,640,64]{2,1,0:T(8,12...) custom-call(f32[96,640]{1,0:T(8,128)} %bitcast.18, ...), custom_call_target="tpu_custom_call" | custom-call | tf_op jit(solution)/shard_map/pallas_call | solution.py:444
  182.7 0.0 copy-start.4
  182.7 1.3 fusion.8
  184.0 1.5 fusion.7
  185.5 0.0 copy-start.3
  185.5 1.9 copy.37
  187.4 1.8 copy.38
  189.2 1.7 copy.45
  190.8 0.0 copy-done.4
  190.8 0.0 copy-start.2
  190.8 0.8 copy.46
  191.6 0.0 copy-done.3
  191.7 0.8 copy.47
  192.5 0.0 copy-done.2
  192.5 0.0 copy-start.1
  192.5 1.1 copy.48
  193.5 0.7 copy-done.1
  194.3 0.0 copy-start
  194.3 1.1 copy.49
  195.3 0.7 copy-done
  196.1 1.1 copy.50
  (3 shorter events, 0.0 us)
Async XLA Ops:
  182.7 8.1 %copy-start.4 = (f32[1,640,256]{2,1,0:T(8,128)S(1)}, f32[1,640,256]{2,1,0:T(8,128)}, u32[]{:S(2)}) copy-start(f32[1,640,256]{2,1,0:T(8,128)} %get-tuple-element.92) | copy-start | bytes 1966084
  185.5 6.1 %copy-start.3 = (f32[1,256,640]{2,1,0:T(8,128)S(1)}, f32[1,256,640]{2,1,0:T(8,128)}, u32[]{:S(2)}) copy-start(f32[1,256,640]{2,1,0:T(8,128)} %get-tuple-element.95) | copy-start | bytes 1966084
  190.8 1.7 copy-start.2
  192.5 1.8 copy-start.1
  194.3 1.8 copy-start

commit v3 on v2

--- a/solution.py
+++ b/solution.py
@@ -78,8 +78,9 @@
     tp, dp, inside,
     x_ref, valid_ref, bias_ref, cos_ref, sin_ref,
     g_attn, g_q, g_k, wq, wk, wv, wo, g_pa, g_ff, wg, wu, wd, g_pf,
-    sect_out, gains_out, dwq, dwk, dwv, dwo, dwg, dwu, dwd,
-    wkv_all, wkf, wvf, hbuf, xbuf, sbuf,
+    sect_out, gains_out, owq, owk, owv, owo, owg, owu, owd,
+    dwq, dwo, dwg, dwu, dwd,
+    wkf, wvf, hbuf, xbuf, sbuf,
     a_all, b_all, df_all, do_all,
     o_send, o_recv, f_send, f_recv, db_send, db_recv, da_send, da_recv, kv_send, kv_recv,
     qn_s, qi_s, kn_s, ki_s, qr_s, kr_s, v_s, p_s, att_s,
@@ -90,9 +91,14 @@
     me = lax.axis_index("tp")
     other = 1 - sec
     rows, width = x_ref.shape
-    cols = wk.shape[1]
+    cols = wk.shape[0]
     scale = g_q.shape[1] ** (-0.5)
-    peers = [lax.rem(me + k, tp) for k in range(tp)]
+    if tp == 4:
+        first = me + 1 - 2 * lax.rem(me, 2)
+        second = me + 2 - 4 * lax.rem(me // 2, 2)
+        peers = [me, 3 - me, first, second]
+    else:
+        peers = [lax.rem(me + k, tp) for k in range(tp)]
     mine = pl.ds(pl.multiple_of(me * rows, 16), rows)
 
     barrier = pltpu.get_barrier_semaphore()
@@ -148,71 +154,85 @@
 
     if inside:
         dkv_s, gain_tp, gain_dp, d_send, d_recv, g_send, g_recv = dp_refs[-7:]
-        low, high = lax.rem(z, 2), lax.rem(z // 2, 2)
-        near, far = z + 1 - 2 * low, z + 2 - 4 * high
+        middle = jnp.logical_and(z >= 1, z <= 2)
+        edge = jnp.logical_not(middle)
+        near = z + 1 - 2 * lax.rem(z, 2)
+        across = 3 - z
+        side = lax.rem(z + 1, 2)
         grads = [dwd.at[0], dwg.at[0], dwu.at[0], dwo.at[0], dwq.at[0], dkv_s]
-        live = {}
+        finals = [owd, owg, owu, owo, owq]
 
         def place(ref, start, size):
             return ref.at[pl.ds(pl.multiple_of(start, 16), size)]
 
         def move(i, step, src, dst, peer):
-            c = pltpu.make_async_remote_copy(
+            return pltpu.make_async_remote_copy(
                 src_ref=src, dst_ref=dst, send_sem=d_send.at[i, step], recv_sem=d_recv.at[i, step],
                 device_id={"dp": peer}, device_id_type=MESH,
             )
-            c.start()
-            pending.append(c)
-            live[i] = c
+
+        plan = []
+        for i in range(6):
+            all_out, all_in, half_out, half_in, whole = dp_refs[5 * i:5 * i + 5]
+            half = whole.shape[0] // 2
+            done = place(whole, side * half, half)
+            plan.append((
+                move(i, 0, all_out, all_in, near), move(i, 1, half_out, half_in, across),
+                move(i, 2, done, done, across), move(i, 3, whole, whole, near),
+            ))
 
         def advance(step, *which):
             for i in which:
                 acc = grads[i]
-                first_out, first_in, second_out, second_in, whole = dp_refs[5 * i:5 * i + 5]
-                half, quarter = acc.shape[0] // 2, acc.shape[0] // 4
-                own_half = low * half
-                own_quarter = own_half + high * quarter
-                if step > 0:
-                    live[i].wait_recv()
-                if step == 0:
-                    first_out[...] = place(acc, (1 - low) * half, half)[...].astype(BF16)
-                    move(i, 0, first_out, first_in, near)
-                elif step == 1:
-                    kept = place(acc, own_half, half)
-                    kept[...] = kept[...] + first_in[...].astype(F32)
-                    second_out[...] = place(acc, own_half + (1 - high) * quarter, quarter)[...].astype(BF16)
-                    move(i, 1, second_out, second_in, far)
-                elif step == 2:
-                    done = place(whole, own_quarter, quarter)
-                    done[...] = (place(acc, own_quarter, quarter)[...] + second_in[...].astype(F32)).astype(BF16)
-                    move(i, 2, done, done, far)
-                elif step == 3:
-                    done = place(whole, own_half, half)
-                    move(i, 3, done, done, near)
-                elif i < 5:
-                    acc[...] = whole[...].astype(F32)
-                else:
-                    dwk[0] = whole[:, :cols].astype(F32)
-                    dwv[0] = whole[:, cols:].astype(F32)
+                all_out, all_in, half_out, half_in, whole = dp_refs[5 * i:5 * i + 5]
+                half = whole.shape[0] // 2
+                c = plan[i]
+
+                @pl.when(edge)
+                def _():
+                    if step == 0:
+                        all_out[...] = acc[...].astype(BF16)
+                        c[0].start()
+                    elif step == 4:
+                        c[3].wait_recv()
+
+                @pl.when(middle)
+                def _():
+                    if step == 1:
+                        c[0].wait_recv()
+                        acc[...] = acc[...] + all_in[...].astype(F32)
+                        half_out[...] = place(acc, (1 - side) * half, half)[...].astype(BF16)
+                        c[1].start()
+                    elif step == 2:
+                        c[1].wait_recv()
+                        place(whole, side * half, half)[...] = (
+                            place(acc, side * half, half)[...] + half_in[...].astype(F32)
+                        ).astype(BF16)
+                        c[2].start()
+                    elif step == 3:
+                        c[2].wait_recv()
+                        c[3].start()
+
+                if step == 4:
+                    if i < 5:
+                        finals[i][0] = whole[...]
+                    else:
+                        owk[0] = whole[:cols]
+                        owv[0] = whole[cols:]
     else:
         dkv_s = dp_refs[0]
 
         def advance(step, *which):
             pass
 
-    wkv_all[me] = jnp.concatenate([wk[...], wv[...]], axis=1)
-    kvw = spread(0, wkv_all, me)
+    own_cols = pl.ds(pl.multiple_of(me * cols, 16), cols)
+    wkf[own_cols] = wk[...]
+    wvf[own_cols] = wv[...]
 
     cross = pltpu.make_async_remote_copy(
         src_ref=sbuf, dst_ref=xbuf, send_sem=x_send_sem, recv_sem=x_recv_sem,
         device_id={"section": other}, device_id_type=MESH,
     )
-
-    arrived(kvw)
-    for j in range(tp):
-        block = wkv_all[j]
-        wkf[:, j * cols:(j + 1) * cols] = block[:, :cols]
-        wvf[:, j * cols:(j + 1) * cols] = block[:, cols:]
 
     @pl.when(sec == 0)
     def _():
@@ -226,18 +246,21 @@
     h = hbuf[...]
     n_in, i_in = stats(h)
     a_all[mine] = (n_in * g_attn[...]).astype(BF16)
-    arrived(spread(1, a_all, mine))
+    a_copies = spread(1, a_all, mine)
+    kvw = spread(0, wkf, own_cols) + spread(10, wvf, own_cols)
+    arrived(a_copies)
     a = a_all[...]
     cos, sin = cos_ref[...], sin_ref[...]
     qn, qi = stats(dot(a, wq[...]))
     qn_s[...] = qn
     qi_s[...] = qi
     qr_s[...] = rotate(qn * g_q[...], cos, sin).astype(BF16)
-    kn, ki = stats(dot(a, wkf[...]).astype(BF16).astype(F32))
+    arrived(kvw)
+    kn, ki = stats(dot_nt(a, wkf[...]).astype(BF16).astype(F32))
     kn_s[...] = kn
     ki_s[...] = ki
     kr_s[...] = rotate(kn * g_k[...], cos, sin).astype(BF16)
-    v_s[...] = dot(a, wvf[...]).astype(BF16)
+    v_s[...] = dot_nt(a, wvf[...]).astype(BF16)
     s = dot_nt(qr_s[...], kr_s[...]) * scale + bias_ref[...]
     e = jnp.exp(s - jnp.max(s, axis=-1, keepdims=True))
     p = e / jnp.sum(e, axis=-1, keepdims=True)
@@ -276,7 +299,7 @@
 
     @pl.when(sec == 1)
     def _():
-        sect_out[...] = out
+        sect_out[0] = out
         hbuf[...] = x_ref[...] * valid_ref[...]
 
     up_g = hbuf[...]
@@ -319,7 +342,7 @@
     dv_s[...] = dv.astype(BF16)
     da_copies = scatter(
         8, da_send, da_recv,
-        lambda at: dot_nt(dq_s[at], wq[...]) + dot_nt(dk_s[at], wkf[...]) + dot_nt(dv_s[at], wvf[...]),
+        lambda at: dot_nt(dq_s[at], wq[...]) + dot(dk_s[at], wkf[...]) + dot(dv_s[at], wvf[...]),
     )
     for j in range(tp):
         kv_send[j] = jnp.concatenate(
@@ -333,7 +356,6 @@
     pending.extend(kv_copies)
     dwo[0] = dot_tn(att_s[...], do_all[...])
     advance(0, 3)
-    advance(1, 0, 1, 2)
     da = total(da_copies, da_recv)
     in_back, dg_attn = norm_back(n_in, i_in, g_attn[...], da)
     dh = dmid_s[...] + in_back
@@ -345,7 +367,7 @@
 
     @pl.when(sec == 0)
     def _():
-        sect_out[...] = dh
+        sect_out[0] = dh
 
     zero = jnp.zeros((1, width - dg_q.shape[1] - dg_k.shape[1]), F32)
     gains = jnp.concatenate(
@@ -370,11 +392,13 @@
     for k in range(1, tp):
         kv_copies[k - 1].wait_recv()
         dkv = dkv + kv_recv[k - 1].astype(F32)
-    dkv_s[...] = dot_tn(a_all[...], dkv.astype(BF16))
+    dkv_s[...] = dot_tn(dkv.astype(BF16), a_all[...])
     advance(0, 5)
     if inside:
-        advance(2, 0, 1, 2)
-        advance(1, 3)
+        advance(1, 0, 1)
+        advance(2, 0)
+        advance(1, 2)
+        advance(2, 1)
         for c in gain_copies:
             c.wait_recv()
         gain_dp[z] = sum(gain_tp[j] for j in range(tp))
@@ -388,20 +412,53 @@
             c.start()
             more.append(c)
         pending.extend(gain_copies + more)
-        advance(1, 4, 5)
-        advance(3, 0, 1, 2)
-        advance(2, 3, 4, 5)
-        advance(3, 3, 4, 5)
+        advance(3, 0)
+        advance(2, 2)
+        advance(1, 3)
+        advance(3, 1)
+        advance(2, 3)
+        advance(1, 4)
+        advance(3, 2)
+        advance(2, 4)
+        advance(1, 5)
+        advance(3, 3)
+        advance(2, 5)
+        advance(3, 4)
+        advance(3, 5)
         for c in more:
             c.wait_recv()
         gains_out[...] = sum(gain_dp[j] for j in range(dp))
         advance(4, 0, 1, 2, 3, 4, 5)
     else:
-        dwk[0] = dkv_s[:, :cols]
-        dwv[0] = dkv_s[:, cols:]
+        owk[0] = dkv_s[:cols].astype(BF16)
+        owv[0] = dkv_s[cols:].astype(BF16)
+        for final, grad in ((owq, dwq), (owo, dwo), (owg, dwg), (owu, dwu), (owd, dwd)):
+            final[...] = grad[...].astype(BF16)
     for c in pending:
         c.wait_send()
     cross.wait_send()
+    if inside:
+        @pl.when(edge)
+        def _():
+            for c in plan:
+                c[0].wait_send()
+
+        @pl.when(middle)
+        def _():
+            for c in plan:
+                for step in (1, 2, 3):
+                    c[step].wait_send()
+
+
+def finish_kernel(hd, sect, gains, *refs):
+    mats, out, outs = refs[:7], refs[7], refs[8:]
+    out[...] = sect[...]
+    for i in range(4):
+        outs[i][...] = gains[i:i + 1]
+    outs[4][...] = gains[4:5, :hd]
+    outs[5][...] = gains[4:5, hd:2 * hd]
+    for m, o in zip(mats, outs[6:]):
+        o[...] = m[...].astype(F32)
 
 
 def local(
@@ -431,28 +488,29 @@
     vm = pltpu.VMEM
     rs = lambda: vm((tp - 1, rows, width), BF16)
     ag = lambda: vm((n, width), BF16)
-    across = [vm((width, 2 * cols), F32)]
+    across = [vm((2 * cols, width), F32)]
     if inside:
         across = []
-        for m, w in ((ff, width), (width, ff), (width, ff), (hd, width), (width, hd), (width, 2 * cols)):
-            across += [vm((m // 2, w), BF16)] * 2 + [vm((m // 4, w), BF16)] * 2 + [vm((m, w), BF16)]
+        for m, w in ((ff, width), (width, ff), (width, ff), (hd, width), (width, hd), (2 * cols, width)):
+            across += [vm((m, w), BF16)] * 2 + [vm((m // 2, w), BF16)] * 2 + [vm((m, w), BF16)]
         sem = pltpu.SemaphoreType.DMA
         across += [
-            vm((width, 2 * cols), F32), vm((tp, 8, width), F32), vm((dp, 8, width), F32),
+            vm((2 * cols, width), F32), vm((tp, 8, width), F32), vm((dp, 8, width), F32),
             sem((6, 4)), sem((6, 4)), sem((2, max(tp, dp) - 1)), sem((2, max(tp, dp) - 1)),
         ]
+    shapes = [
+        (1, width, hd), (1, cols, width), (1, cols, width), (1, hd, width), (1, width, ff),
+        (1, width, ff), (1, ff, width),
+    ]
     outs = pl.pallas_call(
         functools.partial(layer_kernel, tp, dp, inside),
         out_shape=[
-            sds((rows, width), F32), sds((8, width), F32),
-            sds((1, width, hd), F32), sds((1, width, cols), F32), sds((1, width, cols), F32),
-            sds((1, hd, width), F32), sds((1, width, ff), F32), sds((1, width, ff), F32),
-            sds((1, ff, width), F32),
-        ],
+            sds((1, rows, width), F32), sds((8, width), F32),
+        ] + [sds(shape, BF16) for shape in shapes],
         in_specs=[pl.BlockSpec(memory_space=pltpu.VMEM)] * 18,
         out_specs=[pl.BlockSpec(memory_space=pltpu.VMEM)] * 9,
-        scratch_shapes=[
-            vm((tp, width, 2 * cols), BF16), vm((width, hd), BF16), vm((width, hd), BF16),
+        scratch_shapes=[vm(shapes[i], F32) for i in (0, 3, 4, 5, 6)] + [
+            vm((hd, width), BF16), vm((hd, width), BF16),
             vm((rows, width), F32), vm((rows, width), F32), vm((rows, width), F32),
             ag(), ag(), ag(), ag(),
             rs(), rs(), rs(), rs(), rs(), rs(), rs(), rs(),
@@ -462,25 +520,33 @@
             vm((n, ff), F32), vm((n, ff), F32), vm((n, ff), F32), vm((n, ff), BF16), vm((n, ff), F32),
             vm((n, ff), BF16), vm((n, ff), BF16), vm((n, hd), BF16), vm((n, hd), BF16), vm((n, hd), BF16),
             vm((rows, width), F32), vm((rows, width), F32),
-            pltpu.SemaphoreType.DMA((10, tp - 1)), pltpu.SemaphoreType.DMA((10, tp - 1)),
+            pltpu.SemaphoreType.DMA((11, tp - 1)), pltpu.SemaphoreType.DMA((11, tp - 1)),
             pltpu.SemaphoreType.DMA, pltpu.SemaphoreType.DMA,
         ] + across,
         compiler_params=pltpu.CompilerParams(
             collective_id=0, has_side_effects=True, vmem_limit_bytes=56 * 1024 * 1024
         ),
     )(
-        x, valid, bias, cos, sin, attn_norm, q_norm, k_norm, w_query[0], w_key[0], w_value[0],
+        x, valid, bias, cos, sin, attn_norm, q_norm, k_norm, w_query[0], w_key[0].T, w_value[0].T,
         w_out[0], post_attn_norm, ff_norm, w_gate[0], w_up[0], w_down[0], post_ff_norm,
     )
     section_out, gains = outs[0], outs[1]
-    mats = list(outs[2:])
+    mats = outs[2:]
     if not inside:
         gains = lax.psum(gains, ("dp", "tp"))
-        mats = [m.astype(F32) for m in lax.psum(tuple(m.astype(BF16) for m in mats), "dp")]
-    row = lambda i: gains[i:i + 1]
+        mats = lax.psum(tuple(mats), "dp")
+    ends = pl.pallas_call(
+        functools.partial(finish_kernel, hd),
+        out_shape=[sds((1, rows, width), F32)] + [sds((1, width), F32)] * 4 + [sds((1, hd), F32)] * 2
+        + [sds(shape, F32) for shape in shapes],
+        in_specs=[pl.BlockSpec(memory_space=pltpu.VMEM)] * 9,
+        out_specs=[pl.BlockSpec(memory_space=pltpu.VMEM)] * 14,
+        compiler_params=pltpu.CompilerParams(vmem_limit_bytes=32 * 1024 * 1024),
+    )(section_out, gains, *mats)
+    g_attn, g_pa, g_ff, g_pf, g_q, g_k, wq, wk, wv, wo, wg, wu, wd = ends[1:]
     return (
-        section_out[None], row(0), gains[4:5, :hd], gains[4:5, hd:2 * hd],
-        mats[0], mats[1], mats[2], mats[3], row(1), row(2), mats[4], mats[5], mats[6], row(3),
+        ends[0], g_attn, g_q, g_k, wq, jnp.swapaxes(wk, 1, 2), jnp.swapaxes(wv, 1, 2), wo, g_pa,
+        g_ff, wg, wu, wd, g_pf,
     )
 
 

time: 198 us -> 186 us (0.939)
  local copies, waits for them, and re-layouts: 18.5 us -> 9.36 us
  Pallas kernels: 174 us -> 171 us
    unnamed x20 -> x18, local copies, waits for them, and re-layouts: 15 us -> 8.64 us
    pallas_call x1, Pallas kernels: 174 us -> 168 us  [local(): pl.pallas_call(functools.partial(layer_kernel, tp, dp, inside), out_shape...]
    pallas_call x0 -> x1, Pallas kernels: none -> 2.83 us  [local(): pl.pallas_call(functools.partial(finish_kernel, hd), out_shape=[sds((1, r...]
    slice x2 -> x0, local copies, waits for them, and re-layouts: 2.82 us -> none  [the longest x1 1.47 us: local(): row = lambda i: gains[i:i + 1]]
where the time goes in v3:
time: 186 us; the launch traced here: 185 us
  Pallas kernels  171 us (92%)
  local copies, waits for them, and re-layouts  9.36 us (5%)
  other arithmetic  4.31 us (2%)
    pallas_call x1, Pallas kernels, local(): pl.pallas_call(functools.partial(layer_kernel, tp, dp, inside), out_shape...  168 us
    unnamed x18, local copies, waits for them, and re-layouts  8.64 us

profile of v3, /device:TPU:0, one launch (start us, length us, event | category | flops | bytes accessed | tf_op | source)
XLA Modules:
  0.0 185.3 jit_solution(3268671448765909042)
XLA Ops:
  0.7 0.7 fusion.4
  1.4 0.1 select_reduce_fusion.2
  1.4 0.7 pad_add_fusion
  2.2 0.1 convert_reduce_fusion
  2.3 0.1 select_reduce_fusion.1
  2.4 0.1 fusion.3
  2.4 0.7 copy.30.valid_ref
  3.2 1.5 multiply_sine_fusion
  4.7 1.0 fusion.2.bias_ref
  5.7 168.1 %shard_map.254 = (f32[1,96,640]{2,1,0:T(8,128)}, f32[8,640]{1,0:T(8,128)}, bf16[1,640,256]{2,1,0:T(8,128)(2,1)}, bf16[1,64,640]{2,1,0:T(8,128)(2,1)}, bf16[1,64,...) custom-call(f32[96,640]{1,0:T(8,128)} %bitcast.21, ...), custom_call_target="tpu_custom_call" | custom-call | tf_op jit(solution)/shard_map/pallas_call | solution.py:505
  173.8 0.0 copy-start
  173.8 1.1 copy-done
  174.9 0.0 copy-start.1
  174.9 1.1 copy-done.1
  176.0 0.0 copy-start.2
  176.0 1.1 copy-done.2
  177.1 0.0 copy-start.3
  177.1 1.0 copy-done.3
  178.1 0.0 copy-start.4
  178.1 1.0 copy-done.4
  179.0 0.0 copy-start.5
  179.0 0.9 copy-done.5
  180.0 0.0 copy-start.6
  180.0 0.9 copy-done.6
  180.9 0.0 copy-start.7
  180.9 0.9 copy-done.7
  181.7 0.0 copy-start.8
  181.8 0.7 copy-done.8
  182.5 2.8 %shard_map.255 = (f32[1,96,640]{2,1,0:T(8,128)}, f32[1,640]{1,0:T(1,128)}, f32[1,640]{1,0:T(1,128)}, f32[1,640]{1,0:T(1,128)}, f32[1,640]{1,0:T(1,128)}, /*index...) custom-call(f32[1,96,640]{2,1,0:T(8,128)S(1)} %copy-done.5, ...), custom_call_target="tpu_custom_call" | custom-call | tf_op jit(solution)/shard_map/pallas_call | solution.py:538
  (3 shorter events, 0.0 us)
Async XLA Ops:
  173.8 1.1 copy-start
  174.9 1.1 copy-start.1
  176.0 1.1 copy-start.2
  177.1 1.0 copy-start.3
  178.1 1.0 copy-start.4
  179.0 0.9 copy-start.5
  180.0 0.9 copy-start.6
  180.9 0.9 copy-start.7
  181.7 0.7 copy-start.8
